TPU v7x, 128 devices: a whole 4x4x4 slice. The times are simulated.
128 devices in a mesh: tm: 16 (over y_hi, x, core), cuts: 8 (over y_lo, z).
Axes of the slice: x: 4, y: 4 (y_hi: 2, y_lo: 2; y = y_hi * 2 + y_lo), z: 4, core: 2. Of those that a mesh axis runs over, the one named last changes fastest.
Arguments:
- volume: float32 [32, 64, 24, 1024], P('tm', 'cuts'), may hold values from -6 to 6
- measured: bfloat16 [32, 6, 64, 24, 1024], P('tm', None, 'cuts'), may hold values from -6 to 6
- counts: int32 [32], P('tm'), may hold values from 2 to 6, as said below
- vshift: int32 [32, 6], P('tm'), may hold values from -2 to 2, as said below
- hshift: int32 [32, 6], P('tm'), may hold values from -16 to 16
- angles: int32 [32, 6], P('tm'), may hold values from 0 to 3
- blocks: bfloat16 [4, 1024, 1024], replicated, may hold values from -0.1875 to 0.1875
Outputs:
- gradient: float32 [32, 64, 24, 1024], P('tm', 'cuts')
Inputs may be any that keep to these rules, and one draw needn't show every extreme that they name: `counts`: some frame has exactly 2 live views and another exactly 6. `vshift`: some live view has the shift 2 and another -2.
All inputs are finite; a program needn't handle non-finite values.
Results may differ from a plain program's by a relative error of at most 0.0029.
Values may be sent and summed in bfloat16 or wider, within the bound.
No kernel may reach another device: no remote copies, remote signals or barrier semaphores. Data moves between devices by JAX's collectives and lax.ppermute only.
A program may use at most 64 MiB of HBM per device.

v0:
```python
from functools import partial

import jax
import jax.numpy as jnp
from jax import lax
from jax.sharding import PartitionSpec as P

H = 2
SH = 16


def with_halo(x, sides, width):
    for axis, dim in sides:
        size, length = (lax.axis_size(axis), x.shape[dim])
        up = [(i, (i + 1) % size) for i in range(size - 1)]
        down = [(j, i) for i, j in up]
        last = lax.slice_in_dim(x, length - width, length, axis=dim)
        first = lax.slice_in_dim(x, 0, width, axis=dim)
        before = lax.ppermute(last, axis, up)
        after = lax.ppermute(first, axis, down)
        x = jnp.concatenate([before, x, after], axis=dim)
    return x


def shifted(x, axis, by):
    size = lax.axis_size(axis)
    pairs = [(i, i + by) for i in range(size) if 0 <= i + by < size]
    return lax.ppermute(x, axis, pairs)


def shift_cols(values, amount):
    padded = jnp.pad(values, [(0, 0)] * (values.ndim - 1) + [(SH, SH)])
    return lax.dynamic_slice_in_dim(padded, SH - amount, values.shape[-1], values.ndim - 1)


def view_residual(
    extended, measured_frame, vertical, lateral, angle_ids, blocks, count, masked, view_no, totals
):
    slices = measured_frame.shape[1]
    block = lax.dynamic_index_in_dim(blocks, angle_ids[view_no], 0, keepdims=False)
    offset = H + vertical[view_no]
    lateral_now = lateral[view_no]
    source_frame = lax.dynamic_slice_in_dim(extended, offset, slices, 0)
    image = jnp.dot(
        source_frame.reshape(-1, source_frame.shape[-1]), block, preferred_element_type=jnp.float32
    )
    image = image.reshape(measured_frame.shape[1:])
    seen = lax.dynamic_index_in_dim(measured_frame, view_no, 0, keepdims=False)
    misfit = shift_cols(image, lateral_now) - seen.astype(jnp.float32)
    misfit = misfit * (view_no < count).astype(jnp.float32)
    spread = shift_cols(misfit.astype(jnp.bfloat16), -lateral_now)
    back = lax.dot_general(
        spread.reshape(-1, spread.shape[-1]),
        block,
        (((1,), (1,)), ((), ())),
        preferred_element_type=jnp.float32,
    )
    back = back.reshape(source_frame.shape)
    present_frame = lax.dynamic_slice_in_dim(totals, offset, slices, 0)
    return lax.dynamic_update_slice_in_dim(totals, present_frame + back, offset, 0)


def smooth_weight(differ):
    return differ / jnp.sqrt(differ * differ + 0.25)


def body(volume, measured, counts, vshift, hshift, angles, blocks):
    frames = volume.shape[0]
    slices = volume.shape[1]
    lowered = volume.astype(jnp.bfloat16)
    extended = with_halo(lowered, (("cuts", 1),), H)
    fitted_frames = []
    for frame_number in range(frames):
        extended_frame_index = extended[frame_number]
        empty = jnp.zeros(extended_frame_index.shape, jnp.float32)
        step_forward = partial(
            view_residual,
            extended_frame_index,
            measured[frame_number],
            vshift[frame_number],
            hshift[frame_number],
            angles[frame_number],
            blocks,
            counts[frame_number],
            True,
        )
        totals = lax.fori_loop(0, measured.shape[1], step_forward, empty)
        fitted_frames.append(totals)
    stacked = jnp.stack(fitted_frames)
    lower_rim = stacked[:, :H]
    upper_rim = stacked[:, slices + H :]
    from_above = shifted(lower_rim, "cuts", -1)
    from_below = shifted(upper_rim, "cuts", 1)
    fitted_volume = stacked[:, H : slices + H]
    fitted_volume = fitted_volume.at[:, :H].add(from_below)
    fitted_volume = fitted_volume.at[:, slices - H :].add(from_above)
    total_frames = frames * lax.axis_size("tm")
    first_global = lax.axis_index("tm") * frames
    rimmed = with_halo(volume.astype(jnp.bfloat16), (("tm", 0),), 1).astype(volume.dtype)
    global_no = first_global - 1 + jnp.arange(frames + 1, dtype=jnp.int32)
    valid = ((global_no >= 0) & (global_no + 1 < total_frames)).astype(jnp.float32)
    weight = smooth_weight(rimmed[1:] - rimmed[:-1]) * valid[:, None, None, None]
    varied = weight[:-1] - weight[1:]
    return fitted_volume + 0.5 * varied


def solution(mesh):
    in_specs = (
        P("tm", "cuts", None, None),
        P("tm", None, "cuts", None, None),
        P("tm"),
        P("tm", None),
        P("tm", None),
        P("tm", None),
        P(),
    )
    out_specs = P("tm", "cuts", None, None)
    return jax.shard_map(body, mesh=mesh, in_specs=in_specs, out_specs=out_specs, check_vma=False)
```

profile of v0, /device:TPU:24, one launch (start us, length us, event | category | flops | bytes accessed | tf_op | source)
XLA Modules:
  0.0 210.7 jit_solution(11748359910561422610)
XLA Ops:
  1.6 3.8 %collective-permute-start = (bf16[2,2,24,1024]{3,2,1,0:T(8,128)(2,1)S(1)}, bf16[2,2,24,1024]{3,2,1,0:T(8,128)(2,1)S(1)}, u32[]{:S(2)}, u32[]{:S(2)}) collective-permute-start(bf16[2,2,24,1024]{3,2,1,0:T(8,128)(2,1)S(1)} %get-tuple-element.581), channel_id=1, source_target_pairs={{0,1},{1,2},{2,3},{3,4},{4,5},{5,6},{6,7},{8,9},{9,10},{10,11},{11... | collective-permute-start | bytes 589832 | tf_op jit(solution)/shard_map/ppermute | solution.py:19
  5.4 4.2 %collective-permute-start.1 = (bf16[2,2,24,1024]{3,2,1,0:T(8,128)(2,1)S(1)}, bf16[2,2,24,1024]{3,2,1,0:T(8,128)(2,1)S(1)}, u32[]{:S(2)}, u32[]{:S(2)}) collective-permute-start(bf16[2,2,24,1024]{3,2,1,0:T(8,128)(2,1)S(1)} %get-tuple-element.582), channel_id=1, source_target_pairs={{1,0},{2,1},{3,2},{4,3},{5,4},{6,5},{7,6},{9,8},{10,9},{11,10},{12... | collective-permute-start | bytes 589832 | tf_op jit(solution)/shard_map/ppermute | solution.py:20
  9.7 5.1 %slice_bitcast_fusion = (bf16[6,8,24,1024]{3,2,1,0:T(8,128)(2,1)}, bf16[6,8,24,1024]{3,2,1,0:T(8,128)(2,1)}) fusion(bf16[2,6,8,24,1024]{4,3,2,1,0:T(8,128)(2,1)} %param.16), kind=kLoop, calls=%fused_computation.42 | loop fusion | bytes 9437184 | tf_op jit(solution)/shard_map/squeeze | solution.py:79
  16.7 80.0 %while.34 = (s32[]{:T(128)}, f32[12,24,1024]{2,1,0:T(8,128)S(1)}, s32[6]{0:T(128)S(1)}, bf16[12,24,1024]{2,1,0:T(8,128)(2,1)S(1)}, s32[6]{0:T(128)S(1)}, /*index...) while((s32[]{:T(128)}, f32[12,24,1024]{2,1,0:T(8,128)S(1)}, ...), condition=%wide.region_1.2_spmd, body=%wide.region_0.1_spmd.sunk | while | flops 806289408 | bytes 8913307 | solution.py:87
  27.6 2.5 %fusion.66 = f32[12,24,1024]{2,1,0:T(8,128)S(1)} fusion(f32[12,24,1024]{2,1,0:T(8,128)S(1)} %get-tuple-element.768, s32[]{:T(128)S(6)} %select_n.126, bf16[4,1024,1024]{2,1,0:T(8,128)(2,1)} %get-tuple-element.788, s32[]{:T(128)S(6)} %select_n.127, s32[]{:T(128)S(6)} %select_n.128, bf16[8,24,1024]{2,1,0:T(8,128)(2,1)S(1)} %fusion.65), kind=kOutput, calls=%fused_computation.7.clone.1 | convolution fusion | flops 402849792 | bytes 4063244 | tf_op jit(solution)/shard_map/while/body/eval_jaxpr/dot_general | solution.py:52
  40.9 2.5 %fusion.66 = f32[12,24,1024]{2,1,0:T(8,128)S(1)} fusion(f32[12,24,1024]{2,1,0:T(8,128)S(1)} %get-tuple-element.768, s32[]{:T(128)S(6)} %select_n.126, bf16[4,1024,1024]{2,1,0:T(8,128)(2,1)} %get-tuple-element.788, s32[]{:T(128)S(6)} %select_n.127, s32[]{:T(128)S(6)} %select_n.128, bf16[8,24,1024]{2,1,0:T(8,128)(2,1)S(1)} %fusion.65), kind=kOutput, calls=%fused_computation.7.clone.1 | convolution fusion | flops 402849792 | bytes 4063244 | tf_op jit(solution)/shard_map/while/body/eval_jaxpr/dot_general | solution.py:52
  54.2 2.5 %fusion.66 = f32[12,24,1024]{2,1,0:T(8,128)S(1)} fusion(f32[12,24,1024]{2,1,0:T(8,128)S(1)} %get-tuple-element.768, s32[]{:T(128)S(6)} %select_n.126, bf16[4,1024,1024]{2,1,0:T(8,128)(2,1)} %get-tuple-element.788, s32[]{:T(128)S(6)} %select_n.127, s32[]{:T(128)S(6)} %select_n.128, bf16[8,24,1024]{2,1,0:T(8,128)(2,1)S(1)} %fusion.65), kind=kOutput, calls=%fused_computation.7.clone.1 | convolution fusion | flops 402849792 | bytes 4063244 | tf_op jit(solution)/shard_map/while/body/eval_jaxpr/dot_general | solution.py:52
  67.5 2.5 %fusion.66 = f32[12,24,1024]{2,1,0:T(8,128)S(1)} fusion(f32[12,24,1024]{2,1,0:T(8,128)S(1)} %get-tuple-element.768, s32[]{:T(128)S(6)} %select_n.126, bf16[4,1024,1024]{2,1,0:T(8,128)(2,1)} %get-tuple-element.788, s32[]{:T(128)S(6)} %select_n.127, s32[]{:T(128)S(6)} %select_n.128, bf16[8,24,1024]{2,1,0:T(8,128)(2,1)S(1)} %fusion.65), kind=kOutput, calls=%fused_computation.7.clone.1 | convolution fusion | flops 402849792 | bytes 4063244 | tf_op jit(solution)/shard_map/while/body/eval_jaxpr/dot_general | solution.py:52
  80.9 2.5 %fusion.66 = f32[12,24,1024]{2,1,0:T(8,128)S(1)} fusion(f32[12,24,1024]{2,1,0:T(8,128)S(1)} %get-tuple-element.768, s32[]{:T(128)S(6)} %select_n.126, bf16[4,1024,1024]{2,1,0:T(8,128)(2,1)} %get-tuple-element.788, s32[]{:T(128)S(6)} %select_n.127, s32[]{:T(128)S(6)} %select_n.128, bf16[8,24,1024]{2,1,0:T(8,128)(2,1)S(1)} %fusion.65), kind=kOutput, calls=%fused_computation.7.clone.1 | convolution fusion | flops 402849792 | bytes 4063244 | tf_op jit(solution)/shard_map/while/body/eval_jaxpr/dot_general | solution.py:52
  94.2 2.5 %fusion.66 = f32[12,24,1024]{2,1,0:T(8,128)S(1)} fusion(f32[12,24,1024]{2,1,0:T(8,128)S(1)} %get-tuple-element.768, s32[]{:T(128)S(6)} %select_n.126, bf16[4,1024,1024]{2,1,0:T(8,128)(2,1)} %get-tuple-element.788, s32[]{:T(128)S(6)} %select_n.127, s32[]{:T(128)S(6)} %select_n.128, bf16[8,24,1024]{2,1,0:T(8,128)(2,1)S(1)} %fusion.65), kind=kOutput, calls=%fused_computation.7.clone.1 | convolution fusion | flops 402849792 | bytes 4063244 | tf_op jit(solution)/shard_map/while/body/eval_jaxpr/dot_general | solution.py:52
  96.9 83.8 %while.35 = (s32[]{:T(128)}, f32[12,24,1024]{2,1,0:T(8,128)S(1)}, s32[6]{0:T(128)S(1)}, bf16[12,24,1024]{2,1,0:T(8,128)(2,1)}, s32[6]{0:T(128)S(1)}, /*index=5*/...) while((s32[]{:T(128)}, f32[12,24,1024]{2,1,0:T(8,128)S(1)}, ...), condition=%wide.region_3.4_spmd, body=%wide.region_2.3_spmd.sunk | while | flops 806289408 | bytes 8913307 | solution.py:87
  101.5 2.3 %fusion.70 = f32[8,24,1024]{2,1,0:T(8,128)S(1)} fusion(bf16[4,1024,1024]{2,1,0:T(8,128)(2,1)} %get-tuple-element.740, s32[]{:T(128)S(6)} %select_n.131, bf16[12,24,1024]{2,1,0:T(8,128)(2,1)} %get-tuple-element.738, s32[]{:T(128)S(6)} %select_n.130), kind=kOutput, calls=%fused_computation.19.clone.1 | convolution fusion | flops 402653184 | bytes 3276808 | tf_op jit(solution)/shard_map/while/body/eval_jaxpr/dot_general | solution.py:44
  108.3 2.5 %fusion.72 = f32[12,24,1024]{2,1,0:T(8,128)S(1)} fusion(f32[12,24,1024]{2,1,0:T(8,128)S(1)} %get-tuple-element.720, s32[]{:T(128)S(6)} %select_n.130, bf16[4,1024,1024]{2,1,0:T(8,128)(2,1)} %get-tuple-element.740, s32[]{:T(128)S(6)} %select_n.131, s32[]{:T(128)S(6)} %select_n.132, bf16[8,24,1024]{2,1,0:T(8,128)(2,1)S(1)} %fusion.71), kind=kOutput, calls=%fused_computation.24.clone.1 | convolution fusion | flops 402849792 | bytes 4063244 | tf_op jit(solution)/shard_map/while/body/eval_jaxpr/dot_general | solution.py:52
  115.4 2.3 %fusion.70 = f32[8,24,1024]{2,1,0:T(8,128)S(1)} fusion(bf16[4,1024,1024]{2,1,0:T(8,128)(2,1)} %get-tuple-element.740, s32[]{:T(128)S(6)} %select_n.131, bf16[12,24,1024]{2,1,0:T(8,128)(2,1)} %get-tuple-element.738, s32[]{:T(128)S(6)} %select_n.130), kind=kOutput, calls=%fused_computation.19.clone.1 | convolution fusion | flops 402653184 | bytes 3276808 | tf_op jit(solution)/shard_map/while/body/eval_jaxpr/dot_general | solution.py:44
  122.3 2.5 %fusion.72 = f32[12,24,1024]{2,1,0:T(8,128)S(1)} fusion(f32[12,24,1024]{2,1,0:T(8,128)S(1)} %get-tuple-element.720, s32[]{:T(128)S(6)} %select_n.130, bf16[4,1024,1024]{2,1,0:T(8,128)(2,1)} %get-tuple-element.740, s32[]{:T(128)S(6)} %select_n.131, s32[]{:T(128)S(6)} %select_n.132, bf16[8,24,1024]{2,1,0:T(8,128)(2,1)S(1)} %fusion.71), kind=kOutput, calls=%fused_computation.24.clone.1 | convolution fusion | flops 402849792 | bytes 4063244 | tf_op jit(solution)/shard_map/while/body/eval_jaxpr/dot_general | solution.py:52
  129.4 2.3 %fusion.70 = f32[8,24,1024]{2,1,0:T(8,128)S(1)} fusion(bf16[4,1024,1024]{2,1,0:T(8,128)(2,1)} %get-tuple-element.740, s32[]{:T(128)S(6)} %select_n.131, bf16[12,24,1024]{2,1,0:T(8,128)(2,1)} %get-tuple-element.738, s32[]{:T(128)S(6)} %select_n.130), kind=kOutput, calls=%fused_computation.19.clone.1 | convolution fusion | flops 402653184 | bytes 3276808 | tf_op jit(solution)/shard_map/while/body/eval_jaxpr/dot_general | solution.py:44
  136.3 2.5 %fusion.72 = f32[12,24,1024]{2,1,0:T(8,128)S(1)} fusion(f32[12,24,1024]{2,1,0:T(8,128)S(1)} %get-tuple-element.720, s32[]{:T(128)S(6)} %select_n.130, bf16[4,1024,1024]{2,1,0:T(8,128)(2,1)} %get-tuple-element.740, s32[]{:T(128)S(6)} %select_n.131, s32[]{:T(128)S(6)} %select_n.132, bf16[8,24,1024]{2,1,0:T(8,128)(2,1)S(1)} %fusion.71), kind=kOutput, calls=%fused_computation.24.clone.1 | convolution fusion | flops 402849792 | bytes 4063244 | tf_op jit(solution)/shard_map/while/body/eval_jaxpr/dot_general | solution.py:52
  150.3 2.5 %fusion.72 = f32[12,24,1024]{2,1,0:T(8,128)S(1)} fusion(f32[12,24,1024]{2,1,0:T(8,128)S(1)} %get-tuple-element.720, s32[]{:T(128)S(6)} %select_n.130, bf16[4,1024,1024]{2,1,0:T(8,128)(2,1)} %get-tuple-element.740, s32[]{:T(128)S(6)} %select_n.131, s32[]{:T(128)S(6)} %select_n.132, bf16[8,24,1024]{2,1,0:T(8,128)(2,1)S(1)} %fusion.71), kind=kOutput, calls=%fused_computation.24.clone.1 | convolution fusion | flops 402849792 | bytes 4063244 | tf_op jit(solution)/shard_map/while/body/eval_jaxpr/dot_general | solution.py:52
  164.2 2.5 %fusion.72 = f32[12,24,1024]{2,1,0:T(8,128)S(1)} fusion(f32[12,24,1024]{2,1,0:T(8,128)S(1)} %get-tuple-element.720, s32[]{:T(128)S(6)} %select_n.130, bf16[4,1024,1024]{2,1,0:T(8,128)(2,1)} %get-tuple-element.740, s32[]{:T(128)S(6)} %select_n.131, s32[]{:T(128)S(6)} %select_n.132, bf16[8,24,1024]{2,1,0:T(8,128)(2,1)S(1)} %fusion.71), kind=kOutput, calls=%fused_computation.24.clone.1 | convolution fusion | flops 402849792 | bytes 4063244 | tf_op jit(solution)/shard_map/while/body/eval_jaxpr/dot_general | solution.py:52
  178.2 2.5 %fusion.72 = f32[12,24,1024]{2,1,0:T(8,128)S(1)} fusion(f32[12,24,1024]{2,1,0:T(8,128)S(1)} %get-tuple-element.720, s32[]{:T(128)S(6)} %select_n.130, bf16[4,1024,1024]{2,1,0:T(8,128)(2,1)} %get-tuple-element.740, s32[]{:T(128)S(6)} %select_n.131, s32[]{:T(128)S(6)} %select_n.132, bf16[8,24,1024]{2,1,0:T(8,128)(2,1)S(1)} %fusion.71), kind=kOutput, calls=%fused_computation.24.clone.1 | convolution fusion | flops 402849792 | bytes 4063244 | tf_op jit(solution)/shard_map/while/body/eval_jaxpr/dot_general | solution.py:52
  186.4 7.3 %collective-permute-start.5 = (bf16[1,8,24,1024]{3,2,1,0:T(8,128)(2,1)}, bf16[1,8,24,1024]{3,2,1,0:T(8,128)(2,1)}, u32[]{:S(2)}, u32[]{:S(2)}) collective-permute-start(bf16[1,8,24,1024]{3,2,1,0:T(8,128)(2,1)} %get-tuple-element.580), channel_id=1, source_target_pairs={{8,0},{16,8},{24,16},{32,24},{40,32},{48,40},{56,48},{64,56},{72,6... | collective-permute-start | bytes 1179656 | tf_op jit(solution)/shard_map/ppermute | solution.py:20
  193.8 2.6 %collective-permute-done.2 = f32[2,2,24,1024]{3,2,1,0:T(8,128)} collective-permute-done((f32[2,2,24,1024]{3,2,1,0:T(8,128)}, f32[2,2,24,1024]{3,2,1,0:T(8,128)}, u32[]{:S(2)}, u32[]{:S(2)}) %collective-permute-start.2) | collective-permute-done | bytes 393248 | tf_op jit(solution)/shard_map/ppermute | solution.py:28
  197.5 3.3 %collective-permute-start.3 = (f32[2,2,24,1024]{3,2,1,0:T(8,128)S(1)}, f32[2,2,24,1024]{3,2,1,0:T(8,128)S(1)}, u32[]{:S(2)}, u32[]{:S(2)}) collective-permute-start(f32[2,2,24,1024]{3,2,1,0:T(8,128)S(1)} %get-tuple-element.575), channel_id=1, source_target_pairs={{1,0},{2,1},{3,2},{4,3},{5,4},{6,5},{7,6},{9,8},{10,9},{11,10},{12... | collective-permute-start | bytes 1179656 | tf_op jit(solution)/shard_map/ppermute | solution.py:28
  202.7 6.4 %collective-permute-done.3 = f32[2,2,24,1024]{3,2,1,0:T(8,128)S(1)} collective-permute-done((f32[2,2,24,1024]{3,2,1,0:T(8,128)S(1)}, f32[2,2,24,1024]{3,2,1,0:T(8,128)S(1)}, u32[]{:S(2)}, u32[]{:S(2)}) %collective-permute-start.3) | collective-permute-done | bytes 393248 | tf_op jit(solution)/shard_map/ppermute | solution.py:28
  (93 shorter events, 72.0 us)
Async XLA Ops:
  1.5 14.0 %copy-start = (bf16[2,8,24,1024]{3,2,1,0:T(8,128)(2,1)}, bf16[2,8,24,1024]{3,2,1,0:T(8,128)(2,1)S(1)}, u32[]{:S(2)}) copy-start(bf16[2,8,24,1024]{3,2,1,0:T(8,128)(2,1)S(1)} %convert_element_type.116) | copy-start | bytes 2359300
  1.6 13.9 %collective-permute-start = (bf16[2,2,24,1024]{3,2,1,0:T(8,128)(2,1)S(1)}, bf16[2,2,24,1024]{3,2,1,0:T(8,128)(2,1)S(1)}, u32[]{:S(2)}, u32[]{:S(2)}) collective-permute-start(bf16[2,2,24,1024]{3,2,1,0:T(8,128)(2,1)S(1)} %get-tuple-element.581), channel_id=1, source_target_pairs={{0,1},{1,2},{2,3},{3,4},{4,5},{5,6},{6,7},{8,9},{9,10},{10,11},{11... | collective-permute-start | bytes 589832 | tf_op jit(solution)/shard_map/ppermute | solution.py:19
  5.4 10.1 %collective-permute-start.1 = (bf16[2,2,24,1024]{3,2,1,0:T(8,128)(2,1)S(1)}, bf16[2,2,24,1024]{3,2,1,0:T(8,128)(2,1)S(1)}, u32[]{:S(2)}, u32[]{:S(2)}) collective-permute-start(bf16[2,2,24,1024]{3,2,1,0:T(8,128)(2,1)S(1)} %get-tuple-element.582), channel_id=1, source_target_pairs={{1,0},{2,1},{3,2},{4,3},{5,4},{6,5},{7,6},{9,8},{10,9},{11,10},{12... | collective-permute-start | bytes 589832 | tf_op jit(solution)/shard_map/ppermute | solution.py:20
  9.6 5.1 %copy-start.2 = (s32[2]{0:T(128)S(1)}, s32[2]{0:T(128)}, u32[]{:S(2)}) copy-start(s32[2]{0:T(128)} %param.17) | copy-start | bytes 28
  9.6 5.8 %copy-start.4 = (s32[2,6]{1,0:T(2,128)S(1)}, s32[2,6]{1,0:T(2,128)}, u32[]{:S(2)}) copy-start(s32[2,6]{1,0:T(2,128)} %param.19) | copy-start | bytes 148
  9.7 5.8 %copy-start.5 = (s32[2,6]{1,0:T(2,128)S(1)}, s32[2,6]{1,0:T(2,128)}, u32[]{:S(2)}) copy-start(s32[2,6]{1,0:T(2,128)} %param.20) | copy-start | bytes 148
  9.7 5.8 %copy-start.3 = (s32[2,6]{1,0:T(2,128)S(1)}, s32[2,6]{1,0:T(2,128)}, u32[]{:S(2)}) copy-start(s32[2,6]{1,0:T(2,128)} %param.18) | copy-start | bytes 148
  180.6 2.8 %copy-start.1 = (bf16[2,8,24,1024]{3,2,1,0:T(8,128)(2,1)S(1)}, bf16[2,8,24,1024]{3,2,1,0:T(8,128)(2,1)}, u32[]{:S(2)}) copy-start(bf16[2,8,24,1024]{3,2,1,0:T(8,128)(2,1)} %copy-done) | copy-start | bytes 2359300
  181.4 15.0 %collective-permute-start.2 = (f32[2,2,24,1024]{3,2,1,0:T(8,128)}, f32[2,2,24,1024]{3,2,1,0:T(8,128)}, u32[]{:S(2)}, u32[]{:S(2)}) collective-permute-start(f32[2,2,24,1024]{3,2,1,0:T(8,128)} %fusion.41), channel_id=1, source_target_pairs={{0,1},{1,2},{2,3},{3,4},{4,5},{5,6},{6,7},{8,9},{9,10},{10,11},{11... | collective-permute-start | bytes 1179656 | tf_op jit(solution)/shard_map/ppermute | solution.py:28
  184.5 16.4 %collective-permute-start.4 = (bf16[1,8,24,1024]{3,2,1,0:T(8,128)(2,1)}, bf16[1,8,24,1024]{3,2,1,0:T(8,128)(2,1)S(1)}, u32[]{:S(2)}, u32[]{:S(2)}) collective-permute-start(bf16[1,8,24,1024]{3,2,1,0:T(8,128)(2,1)} %get-tuple-element.579), channel_id=1, source_target_pairs={{0,8},{8,16},{16,24},{24,32},{32,40},{40,48},{48,56},{56,64},{64,7... | collective-permute-start | bytes 1179656 | tf_op jit(solution)/shard_map/ppermute | solution.py:19
  186.4 14.5 %collective-permute-start.5 = (bf16[1,8,24,1024]{3,2,1,0:T(8,128)(2,1)}, bf16[1,8,24,1024]{3,2,1,0:T(8,128)(2,1)}, u32[]{:S(2)}, u32[]{:S(2)}) collective-permute-start(bf16[1,8,24,1024]{3,2,1,0:T(8,128)(2,1)} %get-tuple-element.580), channel_id=1, source_target_pairs={{8,0},{16,8},{24,16},{32,24},{40,32},{48,40},{56,48},{64,56},{72,6... | collective-permute-start | bytes 1179656 | tf_op jit(solution)/shard_map/ppermute | solution.py:20
  197.5 11.6 %collective-permute-start.3 = (f32[2,2,24,1024]{3,2,1,0:T(8,128)S(1)}, f32[2,2,24,1024]{3,2,1,0:T(8,128)S(1)}, u32[]{:S(2)}, u32[]{:S(2)}) collective-permute-start(f32[2,2,24,1024]{3,2,1,0:T(8,128)S(1)} %get-tuple-element.575), channel_id=1, source_target_pairs={{1,0},{2,1},{3,2},{4,3},{5,4},{6,5},{7,6},{9,8},{10,9},{11,10},{12... | collective-permute-start | bytes 1179656 | tf_op jit(solution)/shard_map/ppermute | solution.py:28
where the time goes:
time: 213 us; the launch traced here: 211 us
  loops' own time  69.1 us (32%)
  matrix products  56.7 us (27%)
  local copies, waits for them, and re-layouts  30.6 us (14%)
  starting transfers between devices  22.6 us (11%)
  other arithmetic  22.5 us (11%)
  waiting for transfers between devices  8.96 us (4%)
    another operation x2, loops' own time, body(): totals = lax.fori_loop(0, measured.shape[1], step_forward, empty)  69.1 us
    dot_general x12, matrix products, view_residual(): lax.dot_general(spread.reshape(-1, spread.shape[-1]), block, (((1,), (1,)...  29.7 us
    dot_general x12, matrix products, view_residual(): jnp.dot(source_frame.reshape(-1, source_frame.shape[-1]), block, preferre...  27 us
    convert_element_type x12, other arithmetic, view_residual(): spread = shift_cols(misfit.astype(jnp.bfloat16), -lateral_now)  15.3 us
    ppermute x2, starting transfers between devices, with_halo(): after = lax.ppermute(first, axis, down)  11.5 us
    ppermute x2, waiting for transfers between devices, shifted(): return lax.ppermute(x, axis, pairs)  8.95 us
    dynamic_slice x12, local copies, waits for them, and re-layouts, view_residual(): offset = H + vertical[view_no]  7.67 us
    dynamic_slice x12, local copies, waits for them, and re-layouts, view_residual(): angle_ids[view_no]  7.5 us
  transfers between devices with their start and end apart: 6, of which 2 were waited for; matrix products, arithmetic and copies ran while one was open for 5% of the time, Pallas kernels for 0%

commit v1 on v0

v1 whole, which is shorter than its diff:
```python
import jax
import jax.numpy as jnp
from jax import lax
from jax.experimental import pallas as pl
from jax.experimental.pallas import tpu as pltpu
from jax.sharding import PartitionSpec as P

H = 2
NA = 4
LANES = 128
BF16 = jnp.bfloat16
F32 = jnp.float32
NT = (((1,), (1,)), ((), ()))


def lateral(buf, index, h, width):
    start = pl.multiple_of(jnp.where(h < 0, 0, LANES), LANES)
    part = h & (LANES - 1)
    amount = (LANES - part) & (LANES - 1)
    values = buf[index + (slice(None), pl.ds(start, width + LANES))].astype(F32)
    tiles = width // LANES
    turned = [
        pltpu.roll(values[:, j * LANES : (j + 1) * LANES], amount, 1) for j in range(tiles + 1)
    ]
    lane = lax.broadcasted_iota(jnp.int32, turned[0].shape, 1)
    near = lane < LANES - part
    return jnp.concatenate(
        [jnp.where(near, turned[j], turned[j + 1]) for j in range(tiles)], axis=1
    )


def rim_kernel(
    counts, vshift, hshift, angles, measured, blocks, volume,
    up, down, first, last, edge, table, vol, sums, total, edge_sem, block_sem, vol_sem,
):
    frames, views, slices, rows, width = measured.shape
    inner = pl.ds(LANES, width)
    low_copy = pltpu.make_async_copy(
        measured.at[:, :, 0:H], edge.at[:, :, 0:H, :, inner], edge_sem.at[0])
    high_copy = pltpu.make_async_copy(
        measured.at[:, :, slices - H : slices], edge.at[:, :, H : 2 * H, :, inner], edge_sem.at[1])
    vol_copy = pltpu.make_async_copy(volume, vol, vol_sem)
    block_copies = [
        pltpu.make_async_copy(blocks.at[a], table.at[a], block_sem.at[a]) for a in range(NA)
    ]
    low_copy.start()
    high_copy.start()
    for copy in block_copies:
        copy.start()
    vol_copy.start()
    pad = jnp.zeros((frames, views, 2 * H, rows, LANES), BF16)
    edge[:, :, :, :, 0:LANES] = pad
    edge[:, :, :, :, width + LANES : width + 2 * LANES] = pad
    sums[...] = jnp.zeros_like(sums)
    low_copy.wait()
    high_copy.wait()

    def add_view(i, carry):
        f = i // views
        v = i - f * views
        s = vshift[f, v]
        h = hshift[f, v]
        a = angles[f, v]
        parts = jnp.where(v < counts[f], jnp.abs(s), 0)

        def add_slice(k, carry):
            source = jnp.where(s > 0, 2 * H - s + k, k)
            slot = jnp.where(s > 0, H + k, k + s + H)
            sums[a, f * 2 * H + slot] += lateral(edge, (f, v, source), h, width)
            return carry

        return lax.fori_loop(0, parts, add_slice, carry)

    lax.fori_loop(0, frames * views, add_view, 0)
    for a in range(NA):
        block_copies[a].wait()
        part = (-sums[a]).reshape(frames * 2 * H * rows, width).astype(BF16)
        back = lax.dot_general(part, table[a], NT, preferred_element_type=F32)
        if a == 0:
            total[...] = back
        else:
            total[...] += back
    vol_copy.wait()
    first[...] = vol[0:1].astype(BF16)
    last[...] = vol[1:2].astype(BF16)
    rims = total[...].reshape(frames, 2 * H, rows, width).astype(BF16)
    down[...] = rims[:, 0:H]
    up[...] = rims[:, H : 2 * H]


def fit_kernel(
    counts, vshift, hshift, angles, measured, blocks, volume,
    fit, meas, table, vol, image, sums, live, meas_sem, block_sem, vol_sem,
):
    frames, views, slices, rows, width = measured.shape
    inner = pl.ds(LANES, width)
    n = frames * slices * rows
    vol_copy = pltpu.make_async_copy(volume, vol, vol_sem)
    block_copies = [
        pltpu.make_async_copy(blocks.at[a], table.at[a], block_sem.at[a]) for a in range(NA)
    ]
    meas_copies = [
        pltpu.make_async_copy(measured.at[f, v], meas.at[f, v, :, :, inner], meas_sem.at[f, v])
        for f in range(frames) for v in range(views)
    ]
    vol_copy.start()
    block_copies[0].start()
    per = frames * views // NA
    for a in range(NA):
        for copy in meas_copies[a * per : (a + 1) * per]:
            copy.start()
        if a + 1 < NA:
            block_copies[a + 1].start()
    pad = jnp.zeros((frames, views, slices, rows, LANES), BF16)
    meas[:, :, :, :, 0:LANES] = pad
    meas[:, :, :, :, width + LANES : width + 2 * LANES] = pad
    sums[...] = jnp.zeros_like(sums)
    live[...] = jnp.zeros_like(live)
    here = lax.axis_index("cuts")
    end = lax.axis_size("cuts") * slices
    place = lax.broadcasted_iota(jnp.int32, (slices, width), 0) + here * slices
    lane = lax.broadcasted_iota(jnp.int32, (slices, width), 1)
    vol_copy.wait()
    low = vol[...].reshape(n, width).astype(BF16)
    for a in range(NA):
        block_copies[a].wait()
        for copy in meas_copies[a * per : (a + 1) * per]:
            copy.wait()
        image[a] = jnp.dot(low, table[a], preferred_element_type=F32)
        for i in range(a * per, (a + 1) * per):
            f, v = divmod(i, views)
            s = vshift[f, v]
            h = hshift[f, v]
            slot = jnp.where(v < counts[f], angles[f, v], NA)
            seen = (lane + h >= 0) & (lane + h < width) & (place - s >= 0) & (place - s < end)
            live[f, slot] += jnp.where(seen, 1.0, 0.0)
            for z in range(slices):
                sums[f, slot, H + s + z] += lateral(meas, (f, v, z), h, width)
    for a in range(NA):
        parts = []
        for f in range(frames):
            for z in range(slices):
                at = (f * slices + z) * rows
                scale = live[f, a, z : z + 1, :]
                parts.append(image[a, at : at + rows] * scale - sums[f, a, H + z])
        misfit = jnp.concatenate(parts, axis=0).astype(BF16)
        back = lax.dot_general(misfit, table[a], NT, preferred_element_type=F32)
        back = back.reshape(frames, slices, rows, width)
        if a == 0:
            fit[...] = back
        else:
            fit[...] += back


def weight(differ):
    return differ / jnp.sqrt(differ * differ + 0.25)


def join_kernel(fit, volume, before, after, below, above, out):
    frames, slices = fit.shape[0], fit.shape[1]
    t, c = lax.axis_index("tm"), lax.axis_index("cuts")
    has_before = jnp.where(t > 0, 0.5, 0.0)
    has_after = jnp.where(t < lax.axis_size("tm") - 1, 0.5, 0.0)
    has_below = jnp.where(c > 0, 1.0, 0.0)
    has_above = jnp.where(c < lax.axis_size("cuts") - 1, 1.0, 0.0)
    for z in range(slices):
        edge = [before[0, z].astype(F32)] + [volume[f, z] for f in range(frames)]
        edge.append(after[0, z].astype(F32))
        factor = [has_before] + [0.5] * (frames - 1) + [has_after]
        w = [weight(edge[k + 1] - edge[k]) * factor[k] for k in range(frames + 1)]
        for f in range(frames):
            value = fit[f, z] + (w[f] - w[f + 1])
            if z < H:
                value += below[f, z].astype(F32) * has_below
            if z >= slices - H:
                value += above[f, z - slices + H].astype(F32) * has_above
            out[f, z] = value


def ring(x, axis, by):
    size = lax.axis_size(axis)
    return lax.ppermute(x, axis, [(i, (i + by) % size) for i in range(size)])


def body(volume, measured, counts, vshift, hshift, angles, blocks):
    frames, views, slices, rows, width = measured.shape
    smem = pl.BlockSpec(memory_space=pltpu.SMEM)
    anyw = pl.BlockSpec(memory_space=pl.ANY)
    vmem = pl.BlockSpec(memory_space=pltpu.VMEM)
    shape = jax.ShapeDtypeStruct
    wide = width + 2 * LANES
    dma = pltpu.SemaphoreType.DMA
    up, down, first, last = pl.pallas_call(
        rim_kernel,
        out_shape=[
            shape((frames, H, rows, width), BF16),
            shape((frames, H, rows, width), BF16),
            shape((1, slices, rows, width), BF16),
            shape((1, slices, rows, width), BF16),
        ],
        in_specs=[smem] * 4 + [anyw] * 3,
        out_specs=[vmem] * 4,
        scratch_shapes=[
            pltpu.VMEM((frames, views, 2 * H, rows, wide), BF16),
            pltpu.VMEM(blocks.shape, BF16),
            pltpu.VMEM(volume.shape, F32),
            pltpu.VMEM((NA, frames * 2 * H, rows, width), F32),
            pltpu.VMEM((frames * 2 * H * rows, width), F32),
            dma((2,)),
            dma((NA,)),
            dma,
        ],
        compiler_params=pltpu.CompilerParams(vmem_limit_bytes=48 * 2**20),
        cost_estimate=pl.CostEstimate(
            flops=2 * NA * frames * 2 * H * rows * width * width, bytes_accessed=14 * 2**20,
            transcendentals=0),
        name="rims",
    )(counts, vshift, hshift, angles, measured, blocks, volume)
    below = ring(up, "cuts", 1)
    above = ring(down, "cuts", -1)
    before = ring(last, "tm", 1)
    after = ring(first, "tm", -1)
    fit = pl.pallas_call(
        fit_kernel,
        out_shape=shape(volume.shape, F32),
        in_specs=[smem] * 4 + [anyw] * 3,
        out_specs=vmem,
        scratch_shapes=[
            pltpu.VMEM((frames, views, slices, rows, wide), BF16),
            pltpu.VMEM(blocks.shape, BF16),
            pltpu.VMEM(volume.shape, F32),
            pltpu.VMEM((NA, frames * slices * rows, width), F32),
            pltpu.VMEM((frames, NA + 1, slices + 2 * H, rows, width), F32),
            pltpu.VMEM((frames, NA + 1, slices, width), F32),
            dma((frames, views)),
            dma((NA,)),
            dma,
        ],
        compiler_params=pltpu.CompilerParams(vmem_limit_bytes=60 * 2**20),
        cost_estimate=pl.CostEstimate(
            flops=4 * NA * frames * slices * rows * width * width, bytes_accessed=16 * 2**20,
            transcendentals=0),
        name="fit",
    )(counts, vshift, hshift, angles, measured, blocks, volume)
    return pl.pallas_call(
        join_kernel,
        out_shape=shape(volume.shape, F32),
        in_specs=[vmem] * 6,
        out_specs=vmem,
        compiler_params=pltpu.CompilerParams(vmem_limit_bytes=32 * 2**20),
        name="join",
    )(fit, volume, before, after, below, above)


def solution(mesh):
    in_specs = (
        P("tm", "cuts", None, None),
        P("tm", None, "cuts", None, None),
        P("tm"),
        P("tm", None),
        P("tm", None),
        P("tm", None),
        P(),
    )
    out_specs = P("tm", "cuts", None, None)
    return jax.shard_map(body, mesh=mesh, in_specs=in_specs, out_specs=out_specs, check_vma=False)
```

time: 213 us -> 40.1 us (0.19)
  the two profiles are of different devices: /device:TPU:24 before, /device:TPU:0 now
where the time goes in v1:
time: 40.1 us; the launch traced here: 39.8 us
  Pallas kernels  23.6 us (59%)
  starting transfers between devices  10.6 us (26%)
  local copies, waits for them, and re-layouts  5.5 us (14%)
    pallas_call x1, Pallas kernels, body(): pl.pallas_call(fit_kernel, out_shape=shape(volume.shape, F32), in_specs=[...  14.4 us
    ppermute x4, starting transfers between devices, ring(): return lax.ppermute(x, axis, [(i, (i + by) % size) for i in range(size)])  10.6 us
    pallas_call x1, Pallas kernels, body(): pl.pallas_call(rim_kernel, out_shape=[shape((frames, H, rows, width), BF1...  6.8 us
    unnamed x14, local copies, waits for them, and re-layouts  5.5 us
    pallas_call x1, Pallas kernels, body(): pl.pallas_call(join_kernel, out_shape=shape(volume.shape, F32), in_specs=...  2.42 us
  transfers between devices with their start and end apart: 4, of which 0 were waited for; matrix products, arithmetic and copies ran while one was open for 0% of the time, Pallas kernels for 36%

profile of v1, /device:TPU:0, one launch (start us, length us, event | category | flops | bytes accessed | tf_op | source)
XLA Modules:
  0.0 39.8 jit_solution(12156373816046425404)
XLA Ops:
  0.0 0.0 copy-start
  0.0 1.4 %copy-done = f32[2,8,24,1024]{3,2,1,0:T(8,128)S(1)} copy-done((f32[2,8,24,1024]{3,2,1,0:T(8,128)S(1)}, f32[2,8,24,1024]{3,2,1,0:T(8,128)}, u32[]{:S(2)}) %copy-start) | copy-done | bytes 1572888
  1.4 0.0 copy-start.3
  1.4 0.7 %copy-done.3 = s32[2,6]{1,0:T(2,128)S(1)} copy-done((s32[2,6]{1,0:T(2,128)S(1)}, s32[2,6]{1,0:T(2,128)}, u32[]{:S(2)}) %copy-start.3) | copy-done | bytes 72
  2.1 0.0 copy-start.4
  2.1 0.7 %copy-done.4 = s32[2,6]{1,0:T(2,128)S(1)} copy-done((s32[2,6]{1,0:T(2,128)S(1)}, s32[2,6]{1,0:T(2,128)}, u32[]{:S(2)}) %copy-start.4) | copy-done | bytes 72
  2.8 0.7 %copy-done.5 = s32[2,6]{1,0:T(2,128)S(1)} copy-done((s32[2,6]{1,0:T(2,128)S(1)}, s32[2,6]{1,0:T(2,128)}, u32[]{:S(2)}) %copy-start.5) | copy-done | bytes 72
  3.4 0.0 copy-start.6
  3.4 0.7 %copy-done.6 = s32[2]{0:T(128)S(1)} copy-done((s32[2]{0:T(128)S(1)}, s32[2]{0:T(128)}, u32[]{:S(2)}) %copy-start.6) | copy-done | bytes 32
  4.1 6.8 %rims.1 = (bf16[2,2,24,1024]{3,2,1,0:T(8,128)(2,1)S(1)}, bf16[2,2,24,1024]{3,2,1,0:T(8,128)(2,1)S(1)}, bf16[1,8,24,1024]{3,2,1,0:T(8,128)(2,1)S(1)}, bf16[1,8,24,1024]{3,2,1,0:T(8,128)(2,1)S(1)}) custom-call(s32[2]{0:T(128)S(1)} %copy-done.6, s32[2,6]{1,0:T(2,128)S(1)} %copy-done.3, s32[2,6]{1,0:T(2,128)S(1)} %copy-done.4, s32[2,6]{1,0:T(2,128)S(1)} %copy-done.5, ...), custom_call_target="tpu_custom_call" | custom-call | flops 1610612736 | bytes 14680064 | tf_op jit(solution)/shard_map/rims/pallas_call | solution.py:193
  10.9 2.1 %collective-permute-start.2 = (bf16[2,2,24,1024]{3,2,1,0:T(8,128)(2,1)S(1)}, bf16[2,2,24,1024]{3,2,1,0:T(8,128)(2,1)S(1)}, u32[]{:S(2)}, u32[]{:S(2)}) collective-permute-start(bf16[2,2,24,1024]{3,2,1,0:T(8,128)(2,1)S(1)} %get-tuple-element.11), channel_id=1, source_target_pairs={{0,1},{1,2},{2,3},{3,4},{4,5},{5,6},{6,7},{7,0},{8,9},{9,10},{10,1... | collective-permute-start | bytes 589832 | tf_op jit(solution)/shard_map/ppermute | solution.py:182
  13.0 3.2 %collective-permute-start.3 = (bf16[2,2,24,1024]{3,2,1,0:T(8,128)(2,1)S(1)}, bf16[2,2,24,1024]{3,2,1,0:T(8,128)(2,1)S(1)}, u32[]{:S(2)}, u32[]{:S(2)}) collective-permute-start(bf16[2,2,24,1024]{3,2,1,0:T(8,128)(2,1)S(1)} %get-tuple-element.12), channel_id=1, source_target_pairs={{0,7},{1,0},{2,1},{3,2},{4,3},{5,4},{6,5},{7,6},{8,15},{9,8},{10,9... | collective-permute-start | bytes 589832 | tf_op jit(solution)/shard_map/ppermute | solution.py:182
  16.2 0.0 collective-permute-start
  16.2 0.0 copy-start.1
  16.2 5.4 %collective-permute-start.1 = (bf16[1,8,24,1024]{3,2,1,0:T(8,128)(2,1)S(1)}, bf16[1,8,24,1024]{3,2,1,0:T(8,128)(2,1)S(1)}, u32[]{:S(2)}, u32[]{:S(2)}) collective-permute-start(bf16[1,8,24,1024]{3,2,1,0:T(8,128)(2,1)S(1)} %get-tuple-element.10), channel_id=1, source_target_pairs={{0,120},{8,0},{16,8},{24,16},{32,24},{40,32},{48,40},{56,48},{64,5... | collective-permute-start | bytes 1179656 | tf_op jit(solution)/shard_map/ppermute | solution.py:182
  21.6 14.4 %fit.1 = f32[2,8,24,1024]{3,2,1,0:T(8,128)} custom-call(s32[2]{0:T(128)} %counts.3, s32[2,6]{1,0:T(2,128)} %vshift.3, s32[2,6]{1,0:T(2,128)} %hshift.3, s32[2,6]{1,0:T(2,128)} %angles.3, bf16[2,6,8,24,1024]{4,3,2,1,0:T(8,128)(2,1)} %measured.3, bf16[4,1024,1024]{2,1,0:T(8,128)(2,1)} %blocks.3, f32[2,8,24,1024]{3,2,1,0:T(8,128)} %volume.5), custom_call_target="tpu_custom_call" | custom-call | flops 6442450944 | bytes 16777216 | tf_op jit(solution)/shard_map/fit/pallas_call | solution.py:223
  35.9 0.0 collective-permute-done.2.below
  35.9 0.0 collective-permute-done.3.above
  36.0 0.0 collective-permute-done.before
  36.0 0.0 collective-permute-done.1.after
  36.0 0.0 copy-done.1
  36.0 0.0 copy-start.2
  36.0 1.4 %copy-done.2 = f32[2,8,24,1024]{3,2,1,0:T(8,128)S(1)} copy-done((f32[2,8,24,1024]{3,2,1,0:T(8,128)S(1)}, f32[2,8,24,1024]{3,2,1,0:T(8,128)}, u32[]{:S(2)}) %copy-start.2) | copy-done | bytes 1572888
  37.4 2.4 %join.1 = f32[2,8,24,1024]{3,2,1,0:T(8,128)} custom-call(f32[2,8,24,1024]{3,2,1,0:T(8,128)S(1)} %copy-done.2, f32[2,8,24,1024]{3,2,1,0:T(8,128)S(1)} %copy-done.1, bf16[1,8,24,1024]{3,2,1,0:T(8,128)(2,1)S(1)} %collective-permute-done.before, bf16[1,8,24,1024]{3,2,1,0:T(8,128)(2,1)S(1)} %collective-permute-done.1.after, ...), custom_call_target="tpu_custom_call" | custom-call | tf_op jit(solution)/shard_map/join/pallas_call | solution.py:245
  (1 shorter events, 0.0 us)
Async XLA Ops:
  0.0 1.4 %copy-start = (f32[2,8,24,1024]{3,2,1,0:T(8,128)S(1)}, f32[2,8,24,1024]{3,2,1,0:T(8,128)}, u32[]{:S(2)}) copy-start(f32[2,8,24,1024]{3,2,1,0:T(8,128)} %volume.5) | copy-start | bytes 4718596
  1.4 0.7 %copy-start.3 = (s32[2,6]{1,0:T(2,128)S(1)}, s32[2,6]{1,0:T(2,128)}, u32[]{:S(2)}) copy-start(s32[2,6]{1,0:T(2,128)} %vshift.3) | copy-start | bytes 148
  2.1 0.7 %copy-start.4 = (s32[2,6]{1,0:T(2,128)S(1)}, s32[2,6]{1,0:T(2,128)}, u32[]{:S(2)}) copy-start(s32[2,6]{1,0:T(2,128)} %hshift.3) | copy-start | bytes 148
  2.8 0.7 %copy-start.5 = (s32[2,6]{1,0:T(2,128)S(1)}, s32[2,6]{1,0:T(2,128)}, u32[]{:S(2)}) copy-start(s32[2,6]{1,0:T(2,128)} %angles.3) | copy-start | bytes 148
  3.4 0.7 %copy-start.6 = (s32[2]{0:T(128)S(1)}, s32[2]{0:T(128)}, u32[]{:S(2)}) copy-start(s32[2]{0:T(128)} %counts.3) | copy-start | bytes 28
  10.9 25.0 %collective-permute-start.2 = (bf16[2,2,24,1024]{3,2,1,0:T(8,128)(2,1)S(1)}, bf16[2,2,24,1024]{3,2,1,0:T(8,128)(2,1)S(1)}, u32[]{:S(2)}, u32[]{:S(2)}) collective-permute-start(bf16[2,2,24,1024]{3,2,1,0:T(8,128)(2,1)S(1)} %get-tuple-element.11), channel_id=1, source_target_pairs={{0,1},{1,2},{2,3},{3,4},{4,5},{5,6},{6,7},{7,0},{8,9},{9,10},{10,1... | collective-permute-start | bytes 589832 | tf_op jit(solution)/shard_map/ppermute | solution.py:182
  13.0 23.0 %collective-permute-start.3 = (bf16[2,2,24,1024]{3,2,1,0:T(8,128)(2,1)S(1)}, bf16[2,2,24,1024]{3,2,1,0:T(8,128)(2,1)S(1)}, u32[]{:S(2)}, u32[]{:S(2)}) collective-permute-start(bf16[2,2,24,1024]{3,2,1,0:T(8,128)(2,1)S(1)} %get-tuple-element.12), channel_id=1, source_target_pairs={{0,7},{1,0},{2,1},{3,2},{4,3},{5,4},{6,5},{7,6},{8,15},{9,8},{10,9... | collective-permute-start | bytes 589832 | tf_op jit(solution)/shard_map/ppermute | solution.py:182
  16.2 19.8 %collective-permute-start = (bf16[1,8,24,1024]{3,2,1,0:T(8,128)(2,1)S(1)}, bf16[1,8,24,1024]{3,2,1,0:T(8,128)(2,1)S(1)}, u32[]{:S(2)}, u32[]{:S(2)}) collective-permute-start(bf16[1,8,24,1024]{3,2,1,0:T(8,128)(2,1)S(1)} %get-tuple-element.9), channel_id=1, source_target_pairs={{0,8},{8,16},{16,24},{24,32},{32,40},{40,48},{48,56},{56,64},{64,7... | collective-permute-start | bytes 1179656 | tf_op jit(solution)/shard_map/ppermute | solution.py:182
  16.2 19.8 %copy-start.1 = (f32[2,8,24,1024]{3,2,1,0:T(8,128)S(1)}, f32[2,8,24,1024]{3,2,1,0:T(8,128)}, u32[]{:S(2)}) copy-start(f32[2,8,24,1024]{3,2,1,0:T(8,128)} %volume.5) | copy-start | bytes 4718596
  16.2 19.8 %collective-permute-start.1 = (bf16[1,8,24,1024]{3,2,1,0:T(8,128)(2,1)S(1)}, bf16[1,8,24,1024]{3,2,1,0:T(8,128)(2,1)S(1)}, u32[]{:S(2)}, u32[]{:S(2)}) collective-permute-start(bf16[1,8,24,1024]{3,2,1,0:T(8,128)(2,1)S(1)} %get-tuple-element.10), channel_id=1, source_target_pairs={{0,120},{8,0},{16,8},{24,16},{32,24},{40,32},{48,40},{56,48},{64,5... | collective-permute-start | bytes 1179656 | tf_op jit(solution)/shard_map/ppermute | solution.py:182
  36.0 1.4 %copy-start.2 = (f32[2,8,24,1024]{3,2,1,0:T(8,128)S(1)}, f32[2,8,24,1024]{3,2,1,0:T(8,128)}, u32[]{:S(2)}) copy-start(f32[2,8,24,1024]{3,2,1,0:T(8,128)} %fit.1) | copy-start | bytes 4718596

commit v2 on v1

v2 whole, which is shorter than its diff:
```python
import jax
import jax.numpy as jnp
from jax import lax
from jax.experimental import pallas as pl
from jax.experimental.pallas import tpu as pltpu
from jax.sharding import PartitionSpec as P

H = 2
NA = 4
CHUNKS = 4
LANES = 128
BF16 = jnp.bfloat16
F32 = jnp.float32
NT = (((1,), (1,)), ((), ()))


def lateral(buf, index, h, width):
    start = pl.multiple_of(jnp.where(h < 0, 0, LANES), LANES)
    part = h & (LANES - 1)
    amount = (LANES - part) & (LANES - 1)
    values = buf[index + (slice(None), pl.ds(start, width + LANES))].astype(F32)
    tiles = width // LANES
    turned = [
        pltpu.roll(values[:, j * LANES : (j + 1) * LANES], amount, 1) for j in range(tiles + 1)
    ]
    lane = lax.broadcasted_iota(jnp.int32, turned[0].shape, 1)
    near = lane < LANES - part
    return jnp.concatenate(
        [jnp.where(near, turned[j], turned[j + 1]) for j in range(tiles)], axis=1
    )


def weight(differ):
    return differ * lax.rsqrt(differ * differ + 0.25)


def rim_kernel(
    counts_in, vshift_in, hshift_in, angles_in, measured, blocks, volume,
    up, down, first, last, table, meas, low, vol,
    counts, vshift, hshift, angles, sums, part, total,
    int_sem, meas_sem, block_sem, vol_sem,
):
    frames, views, slices, rows, width = measured.shape
    inner = pl.ds(LANES, width)
    int_copies = [
        pltpu.make_async_copy(a, b, int_sem.at[i])
        for i, (a, b) in enumerate(
            [(counts_in, counts), (vshift_in, vshift), (hshift_in, hshift), (angles_in, angles)])
    ]
    cuts = [(0, H), (slices - H, H), (H, slices - 2 * H)]
    meas_copies = [
        pltpu.make_async_copy(
            measured.at[:, :, z : z + k], meas.at[:, :, z : z + k, :, inner], meas_sem.at[i])
        for i, (z, k) in enumerate(cuts)
    ]
    vol_copy = pltpu.make_async_copy(volume, vol, vol_sem)
    block_copies = [
        pltpu.make_async_copy(blocks.at[a], table.at[a], block_sem.at[a]) for a in range(NA)
    ]
    for copy in int_copies + meas_copies[:2] + block_copies + [vol_copy] + meas_copies[2:]:
        copy.start()
    pad = jnp.zeros((slices, rows, LANES), BF16)
    for f in range(frames):
        for v in range(views):
            meas[f, v, :, :, 0:LANES] = pad
            meas[f, v, :, :, width + LANES : width + 2 * LANES] = pad
    edge = frames * 2 * H * rows
    spare = jnp.zeros((part.shape[1] - edge, width), BF16)
    nothing = jnp.zeros((rows, width), F32)
    for a in range(NA):
        part[a, edge:] = spare
        for k in range(frames * 2 * H):
            sums[a, k] = nothing
    for copy in int_copies + meas_copies[:2]:
        copy.wait()
    for f in range(frames):
        for v in range(views):
            s = vshift[f, v]
            h = hshift[f, v]
            for k in range(H):
                used = (v < counts[f]) & (k < jnp.abs(s))
                a = jnp.where(used, angles[f, v], NA)
                source = jnp.where(used & (s > 0), slices - s + k, k)
                slot = jnp.where(used, jnp.where(s > 0, H + k, H + k + s), 0)
                sums[a, f * 2 * H + slot] += lateral(meas, (f, v, source), h, width)
    pair = 2 * rows
    for a in range(NA):
        for k in range(frames * H):
            part[a, k * pair : (k + 1) * pair] = (
                sums[a, 2 * k : 2 * k + 2].reshape(pair, width).astype(BF16))
    for a in range(NA):
        block_copies[a].wait()
        for c in range(CHUNKS):
            at = slice(c * width // CHUNKS, (c + 1) * width // CHUNKS)
            back = lax.dot_general(table[a, at], part[a], NT, preferred_element_type=F32)
            if a == 0:
                total[at] = back
            else:
                total[at] += back
    vol_copy.wait()
    for f in range(frames):
        for z in range(0, slices, 2):
            at = (f * slices + z) * rows
            low[at : at + pair] = vol[f, z : z + 2].reshape(pair, width).astype(BF16)
    first[...] = vol[0:1].astype(BF16)
    last[...] = vol[frames - 1 : frames].astype(BF16)
    turned = -(total[...].T)
    for f in range(frames):
        at = f * 2 * pair
        down[f] = turned[at : at + pair].reshape(H, rows, width).astype(BF16)
        up[f] = turned[at + pair : at + 2 * pair].reshape(H, rows, width).astype(BF16)
    for copy in meas_copies[2:]:
        copy.wait()


def fit_kernel(
    counts_in, vshift_in, hshift_in, angles_in, meas, table, low, vol,
    fit, counts, vshift, hshift, angles, image, sums, live, misfit, middle, int_sem,
):
    frames, views, slices, rows, wide = meas.shape
    width = wide - 2 * LANES
    int_copies = [
        pltpu.make_async_copy(a, b, int_sem.at[i])
        for i, (a, b) in enumerate(
            [(counts_in, counts), (vshift_in, vshift), (hshift_in, hshift), (angles_in, angles)])
    ]
    for copy in int_copies:
        copy.start()
    nothing = jnp.zeros((rows, width), F32)
    chunk = width // CHUNKS

    def clear(f, a):
        live[f, a] = jnp.zeros((slices, width), F32)
        for z in range(slices):
            sums[f, a, H + z] = nothing

    def add_slice(f, v, z):
        slot = jnp.where(v < counts[f], angles[f, v], NA)
        sums[f, slot, H + vshift[f, v] + z] += lateral(meas, (f, v, z), hshift[f, v], width)

    def add_live(f, v):
        here = lax.axis_index("cuts")
        end = lax.axis_size("cuts") * slices
        place = lax.broadcasted_iota(jnp.int32, (slices, width), 0) + here * slices - vshift[f, v]
        lane = lax.broadcasted_iota(jnp.int32, (slices, width), 1) + hshift[f, v]
        seen = (lane >= 0) & (lane < width) & (place >= 0) & (place < end)
        slot = jnp.where(v < counts[f], angles[f, v], NA)
        live[f, slot] += jnp.where(seen, 1.0, 0.0)

    def make_misfit(a, f, z):
        at = (f * slices + z) * rows
        both = [
            image[a, at + k * rows : at + (k + 1) * rows] * live[f, a, z + k : z + k + 1, :]
            - sums[f, a, H + z + k]
            for k in range(2)
        ]
        misfit[a, at : at + 2 * rows] = jnp.concatenate(both, axis=0).astype(BF16)

    def forward(a, c):
        image[a, :, c * chunk : (c + 1) * chunk] = jnp.dot(
            low[...], table[a, :, c * chunk : (c + 1) * chunk], preferred_element_type=F32)

    def backward(a, c):
        at = slice(c * chunk, (c + 1) * chunk)
        back = lax.dot_general(misfit[a], table[a, at], NT, preferred_element_type=F32)
        if a == 0:
            half = n // frames
            fit[0:half, at] = back[0:half] - middle[:, at]
            fit[half:n, at] = back[half:n] + middle[:, at]
        else:
            fit[:, at] += back

    def add_middle(z):
        middle[z * rows : (z + 1) * rows] = weight(vol[1, z] - vol[0, z]) * 0.5

    n = frames * slices * rows
    clears = [(f, a) for f in range(frames) for a in range(NA)]
    adds = [(f, v, z) for f in range(frames) for v in range(views) for z in range(slices)]
    steps = [(a, c) for a in range(NA) for c in range(CHUNKS)]
    lead = CHUNKS
    for i, step in enumerate(steps):
        forward(*step)
        if i < lead:
            for item in clears[i * len(clears) // lead : (i + 1) * len(clears) // lead]:
                clear(*item)
            for z in range(i * slices // lead, (i + 1) * slices // lead):
                add_middle(z)
        else:
            if i == lead:
                for copy in int_copies:
                    copy.wait()
            k, m = i - lead, len(steps) - lead
            for item in adds[k * len(adds) // m : (k + 1) * len(adds) // m]:
                add_slice(*item)
                if item[2] == 0:
                    add_live(*item[:2])
    pairs = [(f, z) for f in range(frames) for z in range(0, slices, 2)]
    for item in pairs:
        make_misfit(0, *item)
    for a in range(NA):
        for c in range(CHUNKS):
            backward(a, c)
            if a + 1 < NA:
                for item in pairs[c * len(pairs) // CHUNKS : (c + 1) * len(pairs) // CHUNKS]:
                    make_misfit(a + 1, *item)


def join_kernel(fit, volume, before, after, below, above, out, held, sem):
    frames, slices, rows, width = volume.shape
    t, c = lax.axis_index("tm"), lax.axis_index("cuts")
    has_before = jnp.where(t > 0, 0.5, 0.0)
    has_after = jnp.where(t < lax.axis_size("tm") - 1, 0.5, 0.0)
    has_below = jnp.where(c > 0, 1.0, 0.0)
    has_above = jnp.where(c < lax.axis_size("cuts") - 1, 1.0, 0.0)
    copies = []
    for z in range(slices):
        start = weight(volume[0, z] - before[0, z].astype(F32)) * has_before
        stop = weight(after[0, z].astype(F32) - volume[1, z]) * has_after
        for f in range(frames):
            at = (f * slices + z) * rows
            value = fit[at : at + rows] + (start if f == 0 else -stop)
            if z < H:
                value += below[f, z].astype(F32) * has_below
            if z >= slices - H:
                value += above[f, z - slices + H].astype(F32) * has_above
            held[f, z] = value
        copies.append(pltpu.make_async_copy(held.at[:, z], out.at[:, z], sem.at[z]))
        copies[-1].start()
    for copy in copies:
        copy.wait()


def ring(x, axis, by):
    size = lax.axis_size(axis)
    return lax.ppermute(x, axis, [(i, (i + by) % size) for i in range(size)])


def body(volume, measured, counts, vshift, hshift, angles, blocks):
    frames, views, slices, rows, width = measured.shape
    hbm = pl.BlockSpec(memory_space=pltpu.HBM)
    held = pltpu.with_memory_space_constraint
    vmem = pl.BlockSpec(memory_space=pltpu.VMEM)
    shape = jax.ShapeDtypeStruct
    wide = width + 2 * LANES
    dma = pltpu.SemaphoreType.DMA
    n = frames * slices * rows
    edge = pl.cdiv(frames * 2 * H * rows, LANES) * LANES
    ints = [held(x, pltpu.HBM) for x in (counts, vshift, hshift, angles)]
    int_scratch = [pltpu.SMEM(x.shape, jnp.int32) for x in ints]
    up, down, first, last, table, meas, low, vol = pl.pallas_call(
        rim_kernel,
        out_shape=[
            pltpu.VMEM((frames, H, rows, width), BF16),
            pltpu.VMEM((frames, H, rows, width), BF16),
            pltpu.VMEM((1, slices, rows, width), BF16),
            pltpu.VMEM((1, slices, rows, width), BF16),
            pltpu.VMEM(blocks.shape, BF16),
            pltpu.VMEM((frames, views, slices, rows, wide), BF16),
            pltpu.VMEM((n, width), BF16),
            pltpu.VMEM(volume.shape, F32),
        ],
        in_specs=[hbm] * 7,
        out_specs=[vmem] * 8,
        scratch_shapes=int_scratch + [
            pltpu.VMEM((NA + 1, frames * 2 * H, rows, width), F32),
            pltpu.VMEM((NA, edge, width), BF16),
            pltpu.VMEM((width, edge), F32),
            dma((4,)),
            dma((3,)),
            dma((NA,)),
            dma,
        ],
        compiler_params=pltpu.CompilerParams(vmem_limit_bytes=14 * 2**20),
        cost_estimate=pl.CostEstimate(
            flops=2 * NA * edge * width * width, bytes_accessed=16 * 2**20, transcendentals=0),
        name="rims",
    )(*ints, *(held(x, pltpu.HBM) for x in (measured, blocks, volume)))
    below = ring(up, "cuts", 1)
    above = ring(down, "cuts", -1)
    before = ring(last, "tm", 1)
    after = ring(first, "tm", -1)
    fit = pl.pallas_call(
        fit_kernel,
        out_shape=pltpu.VMEM((n, width), F32),
        in_specs=[hbm] * 4 + [vmem] * 4,
        out_specs=vmem,
        scratch_shapes=int_scratch + [
            pltpu.VMEM((NA, n, width), F32),
            pltpu.VMEM((frames, NA + 1, slices + 2 * H, rows, width), F32),
            pltpu.VMEM((frames, NA + 1, slices, width), F32),
            pltpu.VMEM((NA, n, width), BF16),
            pltpu.VMEM((slices * rows, width), F32),
            dma((4,)),
        ],
        compiler_params=pltpu.CompilerParams(vmem_limit_bytes=30 * 2**20),
        cost_estimate=pl.CostEstimate(
            flops=4 * NA * n * width * width, bytes_accessed=16 * 2**20, transcendentals=0),
        name="fit",
    )(*ints, *(held(x, pltpu.VMEM) for x in (meas, table, low, vol)))
    return pl.pallas_call(
        join_kernel,
        out_shape=shape(volume.shape, F32),
        in_specs=[vmem] * 6,
        out_specs=hbm,
        scratch_shapes=[pltpu.VMEM(volume.shape, F32), dma((slices,))],
        compiler_params=pltpu.CompilerParams(vmem_limit_bytes=8 * 2**20),
        name="join",
    )(*(held(x, pltpu.VMEM) for x in (fit, vol, before, after, below, above)))


def solution(mesh):
    in_specs = (
        P("tm", "cuts", None, None),
        P("tm", None, "cuts", None, None),
        P("tm"),
        P("tm", None),
        P("tm", None),
        P("tm", None),
        P(),
    )
    out_specs = P("tm", "cuts", None, None)
    return jax.shard_map(body, mesh=mesh, in_specs=in_specs, out_specs=out_specs, check_vma=False)
```

time: 40.1 us -> 26.3 us (0.66)
  the two profiles are of different devices: /device:TPU:0 before, /device:TPU:7 now
where the time goes in v2:
time: 26.3 us; the launch traced here: 26 us
  Pallas kernels  15.4 us (59%)
  starting transfers between devices  8.3 us (32%)
  waiting for transfers between devices  2.08 us (8%)
    pallas_call x1, Pallas kernels, body(): pl.pallas_call(fit_kernel, out_shape=pltpu.VMEM((n, width), F32), in_spec...  8.7 us
    ppermute x4, starting transfers between devices, ring(): return lax.ppermute(x, axis, [(i, (i + by) % size) for i in range(size)])  8.3 us
    pallas_call x1, Pallas kernels, body(): pl.pallas_call(rim_kernel, out_shape=[pltpu.VMEM((frames, H, rows, width)...  5.4 us
    ppermute x4, waiting for transfers between devices, ring(): return lax.ppermute(x, axis, [(i, (i + by) % size) for i in range(size)])  2.08 us
    pallas_call x1, Pallas kernels, body(): pl.pallas_call(join_kernel, out_shape=shape(volume.shape, F32), in_specs=...  1.29 us
  transfers between devices with their start and end apart: 4, of which 1 were waited for; matrix products, arithmetic and copies ran while one was open for 0% of the time, Pallas kernels for 33%

profile of v2, /device:TPU:7, one launch (start us, length us, event | category | flops | bytes accessed | tf_op | source)
XLA Modules:
  0.0 26.0 jit_solution(11267829896874203372)
XLA Ops:
  0.0 5.4 %rims.1 = (bf16[2,2,24,1024]{3,2,1,0:T(8,128)(2,1)S(1)}, bf16[2,2,24,1024]{3,2,1,0:T(8,128)(2,1)S(1)}, bf16[1,8,24,1024]{3,2,1,0:T(8,128)(2,1)S(1)}, bf16[1,8,24...) custom-call(s32[2]{0:T(128)} %counts_in.3, ...), custom_call_target="tpu_custom_call" | custom-call | flops 2147483648 | bytes 16777216 | tf_op jit(solution)/shard_map/rims/pallas_call | solution.py:250
  5.4 1.7 %collective-permute-start.2 = (bf16[2,2,24,1024]{3,2,1,0:T(8,128)(2,1)S(1)}, bf16[2,2,24,1024]{3,2,1,0:T(8,128)(2,1)S(1)}, u32[]{:S(2)}, u32[]{:S(2)}) collective-permute-start(bf16[2,2,24,1024]{3,2,1,0:T(8,128)(2,1)S(1)} %get-tuple-element.19), channel_id=1, source_target_pairs={{0,1},{1,2},{2,3},{3,4},{4,5},{5,6},{6,7},{7,0},{8,9},{9,10},{10,1... | collective-permute-start | bytes 589832 | tf_op jit(solution)/shard_map/ppermute | solution.py:235
  7.1 3.2 %collective-permute-start.3 = (bf16[2,2,24,1024]{3,2,1,0:T(8,128)(2,1)S(1)}, bf16[2,2,24,1024]{3,2,1,0:T(8,128)(2,1)S(1)}, u32[]{:S(2)}, u32[]{:S(2)}) collective-permute-start(bf16[2,2,24,1024]{3,2,1,0:T(8,128)(2,1)S(1)} %get-tuple-element.20), channel_id=1, source_target_pairs={{0,7},{1,0},{2,1},{3,2},{4,3},{5,4},{6,5},{7,6},{8,15},{9,8},{10,9... | collective-permute-start | bytes 589832 | tf_op jit(solution)/shard_map/ppermute | solution.py:235
  10.3 3.4 %collective-permute-start = (bf16[1,8,24,1024]{3,2,1,0:T(8,128)(2,1)S(1)}, bf16[1,8,24,1024]{3,2,1,0:T(8,128)(2,1)S(1)}, u32[]{:S(2)}, u32[]{:S(2)}) collective-permute-start(bf16[1,8,24,1024]{3,2,1,0:T(8,128)(2,1)S(1)} %get-tuple-element.17), channel_id=1, source_target_pairs={{0,8},{8,16},{16,24},{24,32},{32,40},{40,48},{48,56},{56,64},{64,7... | collective-permute-start | bytes 1179656 | tf_op jit(solution)/shard_map/ppermute | solution.py:235
  13.7 0.0 collective-permute-start.1
  13.7 8.7 %fit.1 = f32[384,1024]{1,0:T(8,128)S(1)} custom-call(s32[2]{0:T(128)} %counts_in.3, s32[2,6]{1,0:T(2,128)} %vshift_in.3, s32[2,6]{1,0:T(2,128)} %hshift_in.3, s32[2,6]{1,0:T(2,128)} %angles_in.3, bf16[2,6,8,24,1280]{4,3,2,1,0:T(8,128)(2,1)S(1)} %get-tuple-element.13.meas, bf16[4,1024,1024]{2,1,0:T(8,128)(2,1)S(1)} %get-tuple-element.14.table, ...), custom_call_target="tpu_custom_call" | custom-call | flops 6442450944 | bytes 16777216 | tf_op jit(solution)/shard_map/fit/pallas_call | solution.py:282
  22.4 0.0 collective-permute-done.2.below
  22.4 0.0 collective-permute-done.3.above
  22.4 0.0 collective-permute-done.before
  22.4 2.1 %collective-permute-done.1.after = bf16[1,8,24,1024]{3,2,1,0:T(8,128)(2,1)S(1)} collective-permute-done((bf16[1,8,24,1024]{3,2,1,0:T(8,128)(2,1)S(1)}, bf16[1,8,24,1024]{3,2,1,0:T(8,128)(2,1)S(1)}, u32[]{:S(2)}, u32[]{:S(2)}) %collective-permute-start.1) | collective-permute-done | bytes 393248 | tf_op jit(solution)/shard_map/ppermute | solution.py:235
  24.5 1.3 %join.1 = f32[2,8,24,1024]{3,2,1,0:T(8,128)} custom-call(f32[384,1024]{1,0:T(8,128)S(1)} %fit.1, f32[2,8,24,1024]{3,2,1,0:T(8,128)S(1)} %get-tuple-element.16.vol.volume, bf16[1,8,24,1024]{3,2,1,0:T(8,128)(2,1)S(1)} %collective-permute-done.before, bf16[1,8,24,1024]{3,2,1,0:T(8,128)(2,1)S(1)} %collective-permute-done.1.after, ...), custom_call_target="tpu_custom_call" | custom-call | tf_op jit(solution)/shard_map/join/pallas_call | solution.py:300
Async XLA Ops:
  5.4 17.0 %collective-permute-start.2 = (bf16[2,2,24,1024]{3,2,1,0:T(8,128)(2,1)S(1)}, bf16[2,2,24,1024]{3,2,1,0:T(8,128)(2,1)S(1)}, u32[]{:S(2)}, u32[]{:S(2)}) collective-permute-start(bf16[2,2,24,1024]{3,2,1,0:T(8,128)(2,1)S(1)} %get-tuple-element.19), channel_id=1, source_target_pairs={{0,1},{1,2},{2,3},{3,4},{4,5},{5,6},{6,7},{7,0},{8,9},{9,10},{10,1... | collective-permute-start | bytes 589832 | tf_op jit(solution)/shard_map/ppermute | solution.py:235
  7.1 15.3 %collective-permute-start.3 = (bf16[2,2,24,1024]{3,2,1,0:T(8,128)(2,1)S(1)}, bf16[2,2,24,1024]{3,2,1,0:T(8,128)(2,1)S(1)}, u32[]{:S(2)}, u32[]{:S(2)}) collective-permute-start(bf16[2,2,24,1024]{3,2,1,0:T(8,128)(2,1)S(1)} %get-tuple-element.20), channel_id=1, source_target_pairs={{0,7},{1,0},{2,1},{3,2},{4,3},{5,4},{6,5},{7,6},{8,15},{9,8},{10,9... | collective-permute-start | bytes 589832 | tf_op jit(solution)/shard_map/ppermute | solution.py:235
  10.3 12.1 %collective-permute-start = (bf16[1,8,24,1024]{3,2,1,0:T(8,128)(2,1)S(1)}, bf16[1,8,24,1024]{3,2,1,0:T(8,128)(2,1)S(1)}, u32[]{:S(2)}, u32[]{:S(2)}) collective-permute-start(bf16[1,8,24,1024]{3,2,1,0:T(8,128)(2,1)S(1)} %get-tuple-element.17), channel_id=1, source_target_pairs={{0,8},{8,16},{16,24},{24,32},{32,40},{40,48},{48,56},{56,64},{64,7... | collective-permute-start | bytes 1179656 | tf_op jit(solution)/shard_map/ppermute | solution.py:235
  13.7 10.8 %collective-permute-start.1 = (bf16[1,8,24,1024]{3,2,1,0:T(8,128)(2,1)S(1)}, bf16[1,8,24,1024]{3,2,1,0:T(8,128)(2,1)S(1)}, u32[]{:S(2)}, u32[]{:S(2)}) collective-permute-start(bf16[1,8,24,1024]{3,2,1,0:T(8,128)(2,1)S(1)} %get-tuple-element.18), channel_id=1, source_target_pairs={{0,120},{8,0},{16,8},{24,16},{32,24},{40,32},{48,40},{56,48},{64,5... | collective-permute-start | bytes 1179656 | tf_op jit(solution)/shard_map/ppermute | solution.py:235

commit v3 on v2

--- a/solution.py
+++ b/solution.py
@@ -102,8 +102,9 @@
         for z in range(0, slices, 2):
             at = (f * slices + z) * rows
             low[at : at + pair] = vol[f, z : z + 2].reshape(pair, width).astype(BF16)
-    first[...] = vol[0:1].astype(BF16)
-    last[...] = vol[frames - 1 : frames].astype(BF16)
+    even = lax.axis_index("tm") % 2 == 0
+    first[...] = vol[pl.ds(jnp.where(even, 0, frames - 1), 1)].astype(BF16)
+    last[...] = vol[pl.ds(jnp.where(even, frames - 1, 0), 1)].astype(BF16)
     turned = -(total[...].T)
     for f in range(frames):
         at = f * 2 * pair
@@ -205,17 +206,21 @@
                     make_misfit(a + 1, *item)
 
 
-def join_kernel(fit, volume, before, after, below, above, out, held, sem):
+def join_kernel(fit, volume, near, far, below, above, out, held, sem):
     frames, slices, rows, width = volume.shape
     t, c = lax.axis_index("tm"), lax.axis_index("cuts")
+    even = t % 2 == 0
     has_before = jnp.where(t > 0, 0.5, 0.0)
     has_after = jnp.where(t < lax.axis_size("tm") - 1, 0.5, 0.0)
     has_below = jnp.where(c > 0, 1.0, 0.0)
     has_above = jnp.where(c < lax.axis_size("cuts") - 1, 1.0, 0.0)
     copies = []
     for z in range(slices):
-        start = weight(volume[0, z] - before[0, z].astype(F32)) * has_before
-        stop = weight(after[0, z].astype(F32) - volume[1, z]) * has_after
+        close, away = near[0, z].astype(F32), far[0, z].astype(F32)
+        before = jnp.where(even, away, close)
+        after = jnp.where(even, close, away)
+        start = weight(volume[0, z] - before) * has_before
+        stop = weight(after - volume[1, z]) * has_after
         for f in range(frames):
             at = (f * slices + z) * rows
             value = fit[at : at + rows] + (start if f == 0 else -stop)
@@ -228,6 +233,14 @@
         copies[-1].start()
     for copy in copies:
         copy.wait()
+
+
+def swap(x, axis, odd):
+    size = lax.axis_size(axis)
+    pairs = {i: i for i in range(size)}
+    for i in range(odd, size - 1, 2):
+        pairs[i], pairs[i + 1] = i + 1, i
+    return lax.ppermute(x, axis, sorted(pairs.items()))
 
 
 def ring(x, axis, by):
@@ -277,8 +290,8 @@
     )(*ints, *(held(x, pltpu.HBM) for x in (measured, blocks, volume)))
     below = ring(up, "cuts", 1)
     above = ring(down, "cuts", -1)
-    before = ring(last, "tm", 1)
-    after = ring(first, "tm", -1)
+    near = swap(last, "tm", 0)
+    far = swap(first, "tm", 1)
     fit = pl.pallas_call(
         fit_kernel,
         out_shape=pltpu.VMEM((n, width), F32),
@@ -305,7 +318,7 @@
         scratch_shapes=[pltpu.VMEM(volume.shape, F32), dma((slices,))],
         compiler_params=pltpu.CompilerParams(vmem_limit_bytes=8 * 2**20),
         name="join",
-    )(*(held(x, pltpu.VMEM) for x in (fit, vol, before, after, below, above)))
+    )(*(held(x, pltpu.VMEM) for x in (fit, vol, near, far, below, above)))
 
 
 def solution(mesh):

time: 26.3 us -> 26.2 us (level)
  starting transfers between devices: 8.3 us -> 10.4 us
  waiting for transfers between devices: 2.08 us -> 0.01 us
    ppermute x0 -> x2, starting transfers between devices: none -> 5.46 us  [swap(): return lax.ppermute(x, axis, sorted(pairs.items()))]
    ppermute x4 -> x2, starting transfers between devices: 8.3 us -> 4.92 us  [ring(): return lax.ppermute(x, axis, [(i, (i + by) % size) for i in range(size)])]
    ppermute x4 -> x2, waiting for transfers between devices: 2.08 us -> 0.01 us  [ring(): return lax.ppermute(x, axis, [(i, (i + by) % size) for i in range(size)])]
  transfers between devices with their start and end apart: 4 -> 4, of which waited for: 1 -> 0; matrix products, arithmetic and copies ran while one was open for 0% -> 0% of each run, Pallas kernels for 33% -> 33%
where the time goes in v3:
time: 26.2 us; the launch traced here: 26.1 us
  Pallas kernels  15.5 us (59%)
  starting transfers between devices  10.4 us (40%)
    pallas_call x1, Pallas kernels, body(): pl.pallas_call(fit_kernel, out_shape=pltpu.VMEM((n, width), F32), in_spec...  8.7 us
    ppermute x2, starting transfers between devices, swap(): return lax.ppermute(x, axis, sorted(pairs.items()))  5.46 us
    pallas_call x1, Pallas kernels, body(): pl.pallas_call(rim_kernel, out_shape=[pltpu.VMEM((frames, H, rows, width)...  5.41 us
    ppermute x2, starting transfers between devices, ring(): return lax.ppermute(x, axis, [(i, (i + by) % size) for i in range(size)])  4.92 us
    pallas_call x1, Pallas kernels, body(): pl.pallas_call(join_kernel, out_shape=shape(volume.shape, F32), in_specs=...  1.36 us
  transfers between devices with their start and end apart: 4, of which 0 were waited for; matrix products, arithmetic and copies ran while one was open for 0% of the time, Pallas kernels for 33%

profile of v3, /device:TPU:7, one launch (start us, length us, event | category | flops | bytes accessed | tf_op | source)
XLA Modules:
  0.0 26.1 jit_solution(2503433879949859083)
XLA Ops:
  0.0 5.4 %rims.1 = (bf16[2,2,24,1024]{3,2,1,0:T(8,128)(2,1)S(1)}, bf16[2,2,24,1024]{3,2,1,0:T(8,128)(2,1)S(1)}, bf16[1,8,24,1024]{3,2,1,0:T(8,128)(2,1)S(1)}, bf16[1,8,24...) custom-call(s32[2]{0:T(128)} %counts_in.3, ...), custom_call_target="tpu_custom_call" | custom-call | flops 2147483648 | bytes 16777216 | tf_op jit(solution)/shard_map/rims/pallas_call | solution.py:263
  5.4 1.7 %collective-permute-start.2 = (bf16[2,2,24,1024]{3,2,1,0:T(8,128)(2,1)S(1)}, bf16[2,2,24,1024]{3,2,1,0:T(8,128)(2,1)S(1)}, u32[]{:S(2)}, u32[]{:S(2)}) collective-permute-start(bf16[2,2,24,1024]{3,2,1,0:T(8,128)(2,1)S(1)} %get-tuple-element.19), channel_id=1, source_target_pairs={{0,1},{1,2},{2,3},{3,4},{4,5},{5,6},{6,7},{7,0},{8,9},{9,10},{10,1... | collective-permute-start | bytes 589832 | tf_op jit(solution)/shard_map/ppermute | solution.py:248
  7.1 3.2 %collective-permute-start.3 = (bf16[2,2,24,1024]{3,2,1,0:T(8,128)(2,1)S(1)}, bf16[2,2,24,1024]{3,2,1,0:T(8,128)(2,1)S(1)}, u32[]{:S(2)}, u32[]{:S(2)}) collective-permute-start(bf16[2,2,24,1024]{3,2,1,0:T(8,128)(2,1)S(1)} %get-tuple-element.20), channel_id=1, source_target_pairs={{0,7},{1,0},{2,1},{3,2},{4,3},{5,4},{6,5},{7,6},{8,15},{9,8},{10,9... | collective-permute-start | bytes 589832 | tf_op jit(solution)/shard_map/ppermute | solution.py:248
  10.3 1.0 %collective-permute-start = (bf16[1,8,24,1024]{3,2,1,0:T(8,128)(2,1)S(1)}, bf16[1,8,24,1024]{3,2,1,0:T(8,128)(2,1)S(1)}, u32[]{:S(2)}, u32[]{:S(2)}) collective-permute-start(bf16[1,8,24,1024]{3,2,1,0:T(8,128)(2,1)S(1)} %get-tuple-element.17), channel_id=1, source_target_pairs={{0,8},{8,0},{16,24},{24,16},{32,40},{40,32},{48,56},{56,48},{64,72... | collective-permute-start | bytes 1179656 | tf_op jit(solution)/shard_map/ppermute | solution.py:243
  11.3 4.5 %collective-permute-start.1 = (bf16[1,8,24,1024]{3,2,1,0:T(8,128)(2,1)S(1)}, bf16[1,8,24,1024]{3,2,1,0:T(8,128)(2,1)S(1)}, u32[]{:S(2)}, u32[]{:S(2)}) collective-permute-start(bf16[1,8,24,1024]{3,2,1,0:T(8,128)(2,1)S(1)} %get-tuple-element.18), channel_id=1, source_target_pairs={{0,0},{8,16},{16,8},{24,32},{32,24},{40,48},{48,40},{56,64},{64,56... | collective-permute-start | bytes 1179656 | tf_op jit(solution)/shard_map/ppermute | solution.py:243
  15.8 8.7 %fit.1 = f32[384,1024]{1,0:T(8,128)S(1)} custom-call(s32[2]{0:T(128)} %counts_in.3, s32[2,6]{1,0:T(2,128)} %vshift_in.3, s32[2,6]{1,0:T(2,128)} %hshift_in.3, s32[2,6]{1,0:T(2,128)} %angles_in.3, bf16[2,6,8,24,1280]{4,3,2,1,0:T(8,128)(2,1)S(1)} %get-tuple-element.13.meas, bf16[4,1024,1024]{2,1,0:T(8,128)(2,1)S(1)} %get-tuple-element.14.table, ...), custom_call_target="tpu_custom_call" | custom-call | flops 6442450944 | bytes 16777216 | tf_op jit(solution)/shard_map/fit/pallas_call | solution.py:295
  24.5 0.0 collective-permute-done.2.below
  24.5 0.0 collective-permute-done.3.above
  24.5 0.0 collective-permute-done.near
  24.5 0.0 collective-permute-done.1.far
  24.5 1.4 %join.1 = f32[2,8,24,1024]{3,2,1,0:T(8,128)} custom-call(f32[384,1024]{1,0:T(8,128)S(1)} %fit.1, f32[2,8,24,1024]{3,2,1,0:T(8,128)S(1)} %get-tuple-element.16.vol.volume, bf16[1,8,24,1024]{3,2,1,0:T(8,128)(2,1)S(1)} %collective-permute-done.near, bf16[1,8,24,1024]{3,2,1,0:T(8,128)(2,1)S(1)} %collective-permute-done.1.far, ...), custom_call_target="tpu_custom_call" | custom-call | tf_op jit(solution)/shard_map/join/pallas_call | solution.py:313
Async XLA Ops:
  5.4 19.1 %collective-permute-start.2 = (bf16[2,2,24,1024]{3,2,1,0:T(8,128)(2,1)S(1)}, bf16[2,2,24,1024]{3,2,1,0:T(8,128)(2,1)S(1)}, u32[]{:S(2)}, u32[]{:S(2)}) collective-permute-start(bf16[2,2,24,1024]{3,2,1,0:T(8,128)(2,1)S(1)} %get-tuple-element.19), channel_id=1, source_target_pairs={{0,1},{1,2},{2,3},{3,4},{4,5},{5,6},{6,7},{7,0},{8,9},{9,10},{10,1... | collective-permute-start | bytes 589832 | tf_op jit(solution)/shard_map/ppermute | solution.py:248
  7.1 17.4 %collective-permute-start.3 = (bf16[2,2,24,1024]{3,2,1,0:T(8,128)(2,1)S(1)}, bf16[2,2,24,1024]{3,2,1,0:T(8,128)(2,1)S(1)}, u32[]{:S(2)}, u32[]{:S(2)}) collective-permute-start(bf16[2,2,24,1024]{3,2,1,0:T(8,128)(2,1)S(1)} %get-tuple-element.20), channel_id=1, source_target_pairs={{0,7},{1,0},{2,1},{3,2},{4,3},{5,4},{6,5},{7,6},{8,15},{9,8},{10,9... | collective-permute-start | bytes 589832 | tf_op jit(solution)/shard_map/ppermute | solution.py:248
  10.3 14.2 %collective-permute-start = (bf16[1,8,24,1024]{3,2,1,0:T(8,128)(2,1)S(1)}, bf16[1,8,24,1024]{3,2,1,0:T(8,128)(2,1)S(1)}, u32[]{:S(2)}, u32[]{:S(2)}) collective-permute-start(bf16[1,8,24,1024]{3,2,1,0:T(8,128)(2,1)S(1)} %get-tuple-element.17), channel_id=1, source_target_pairs={{0,8},{8,0},{16,24},{24,16},{32,40},{40,32},{48,56},{56,48},{64,72... | collective-permute-start | bytes 1179656 | tf_op jit(solution)/shard_map/ppermute | solution.py:243
  11.3 13.3 %collective-permute-start.1 = (bf16[1,8,24,1024]{3,2,1,0:T(8,128)(2,1)S(1)}, bf16[1,8,24,1024]{3,2,1,0:T(8,128)(2,1)S(1)}, u32[]{:S(2)}, u32[]{:S(2)}) collective-permute-start(bf16[1,8,24,1024]{3,2,1,0:T(8,128)(2,1)S(1)} %get-tuple-element.18), channel_id=1, source_target_pairs={{0,0},{8,16},{16,8},{24,32},{32,24},{40,48},{48,40},{56,64},{64,56... | collective-permute-start | bytes 1179656 | tf_op jit(solution)/shard_map/ppermute | solution.py:243

commit v4 on v3

--- a/solution.py
+++ b/solution.py
@@ -177,6 +177,7 @@
     n = frames * slices * rows
     clears = [(f, a) for f in range(frames) for a in range(NA)]
     adds = [(f, v, z) for f in range(frames) for v in range(views) for z in range(slices)]
+    pairs = [(f, z) for f in range(frames) for z in range(0, slices, 2)]
     steps = [(a, c) for a in range(NA) for c in range(CHUNKS)]
     lead = CHUNKS
     for i, step in enumerate(steps):
@@ -190,14 +191,13 @@
             if i == lead:
                 for copy in int_copies:
                     copy.wait()
-            k, m = i - lead, len(steps) - lead
+            k, m = i - lead, len(steps) - lead - 2
             for item in adds[k * len(adds) // m : (k + 1) * len(adds) // m]:
                 add_slice(*item)
                 if item[2] == 0:
                     add_live(*item[:2])
-    pairs = [(f, z) for f in range(frames) for z in range(0, slices, 2)]
-    for item in pairs:
-        make_misfit(0, *item)
+            for item in pairs[max(k - m, 0) * len(pairs) // 2 : max(k - m + 1, 0) * len(pairs) // 2]:
+                make_misfit(0, *item)
     for a in range(NA):
         for c in range(CHUNKS):
             backward(a, c)

time: 26.2 us -> 26.2 us (level)
  no operation moved by 1% of the time
where the time goes in v4:
time: 26.2 us; the launch traced here: 26.1 us
  Pallas kernels  15.5 us (59%)
  starting transfers between devices  10.4 us (40%)
    pallas_call x1, Pallas kernels, body(): pl.pallas_call(fit_kernel, out_shape=pltpu.VMEM((n, width), F32), in_spec...  8.68 us
    ppermute x2, starting transfers between devices, swap(): return lax.ppermute(x, axis, sorted(pairs.items()))  5.46 us
    pallas_call x1, Pallas kernels, body(): pl.pallas_call(rim_kernel, out_shape=[pltpu.VMEM((frames, H, rows, width)...  5.41 us
    ppermute x2, starting transfers between devices, ring(): return lax.ppermute(x, axis, [(i, (i + by) % size) for i in range(size)])  4.92 us
    pallas_call x1, Pallas kernels, body(): pl.pallas_call(join_kernel, out_shape=shape(volume.shape, F32), in_specs=...  1.36 us
  transfers between devices with their start and end apart: 4, of which 0 were waited for; matrix products, arithmetic and copies ran while one was open for 0% of the time, Pallas kernels for 33%

profile of v4, /device:TPU:7, one launch (start us, length us, event | category | flops | bytes accessed | tf_op | source)
XLA Modules:
  0.0 26.1 jit_solution(2503433879949859083)
XLA Ops:
  0.0 5.4 %rims.1 = (bf16[2,2,24,1024]{3,2,1,0:T(8,128)(2,1)S(1)}, bf16[2,2,24,1024]{3,2,1,0:T(8,128)(2,1)S(1)}, bf16[1,8,24,1024]{3,2,1,0:T(8,128)(2,1)S(1)}, bf16[1,8,24...) custom-call(s32[2]{0:T(128)} %counts_in.3, ...), custom_call_target="tpu_custom_call" | custom-call | flops 2147483648 | bytes 16777216 | tf_op jit(solution)/shard_map/rims/pallas_call | solution.py:263
  5.4 1.7 %collective-permute-start.2 = (bf16[2,2,24,1024]{3,2,1,0:T(8,128)(2,1)S(1)}, bf16[2,2,24,1024]{3,2,1,0:T(8,128)(2,1)S(1)}, u32[]{:S(2)}, u32[]{:S(2)}) collective-permute-start(bf16[2,2,24,1024]{3,2,1,0:T(8,128)(2,1)S(1)} %get-tuple-element.19), channel_id=1, source_target_pairs={{0,1},{1,2},{2,3},{3,4},{4,5},{5,6},{6,7},{7,0},{8,9},{9,10},{10,1... | collective-permute-start | bytes 589832 | tf_op jit(solution)/shard_map/ppermute | solution.py:248
  7.1 3.2 %collective-permute-start.3 = (bf16[2,2,24,1024]{3,2,1,0:T(8,128)(2,1)S(1)}, bf16[2,2,24,1024]{3,2,1,0:T(8,128)(2,1)S(1)}, u32[]{:S(2)}, u32[]{:S(2)}) collective-permute-start(bf16[2,2,24,1024]{3,2,1,0:T(8,128)(2,1)S(1)} %get-tuple-element.20), channel_id=1, source_target_pairs={{0,7},{1,0},{2,1},{3,2},{4,3},{5,4},{6,5},{7,6},{8,15},{9,8},{10,9... | collective-permute-start | bytes 589832 | tf_op jit(solution)/shard_map/ppermute | solution.py:248
  10.3 1.0 %collective-permute-start = (bf16[1,8,24,1024]{3,2,1,0:T(8,128)(2,1)S(1)}, bf16[1,8,24,1024]{3,2,1,0:T(8,128)(2,1)S(1)}, u32[]{:S(2)}, u32[]{:S(2)}) collective-permute-start(bf16[1,8,24,1024]{3,2,1,0:T(8,128)(2,1)S(1)} %get-tuple-element.17), channel_id=1, source_target_pairs={{0,8},{8,0},{16,24},{24,16},{32,40},{40,32},{48,56},{56,48},{64,72... | collective-permute-start | bytes 1179656 | tf_op jit(solution)/shard_map/ppermute | solution.py:243
  11.3 4.5 %collective-permute-start.1 = (bf16[1,8,24,1024]{3,2,1,0:T(8,128)(2,1)S(1)}, bf16[1,8,24,1024]{3,2,1,0:T(8,128)(2,1)S(1)}, u32[]{:S(2)}, u32[]{:S(2)}) collective-permute-start(bf16[1,8,24,1024]{3,2,1,0:T(8,128)(2,1)S(1)} %get-tuple-element.18), channel_id=1, source_target_pairs={{0,0},{8,16},{16,8},{24,32},{32,24},{40,48},{48,40},{56,64},{64,56... | collective-permute-start | bytes 1179656 | tf_op jit(solution)/shard_map/ppermute | solution.py:243
  15.8 8.7 %fit.1 = f32[384,1024]{1,0:T(8,128)S(1)} custom-call(s32[2]{0:T(128)} %counts_in.3, s32[2,6]{1,0:T(2,128)} %vshift_in.3, s32[2,6]{1,0:T(2,128)} %hshift_in.3, s32[2,6]{1,0:T(2,128)} %angles_in.3, bf16[2,6,8,24,1280]{4,3,2,1,0:T(8,128)(2,1)S(1)} %get-tuple-element.13.meas, bf16[4,1024,1024]{2,1,0:T(8,128)(2,1)S(1)} %get-tuple-element.14.table, ...), custom_call_target="tpu_custom_call" | custom-call | flops 6442450944 | bytes 16777216 | tf_op jit(solution)/shard_map/fit/pallas_call | solution.py:295
  24.5 0.0 collective-permute-done.2.below
  24.5 0.0 collective-permute-done.3.above
  24.5 0.0 collective-permute-done.near
  24.5 0.0 collective-permute-done.1.far
  24.5 1.4 %join.1 = f32[2,8,24,1024]{3,2,1,0:T(8,128)} custom-call(f32[384,1024]{1,0:T(8,128)S(1)} %fit.1, f32[2,8,24,1024]{3,2,1,0:T(8,128)S(1)} %get-tuple-element.16.vol.volume, bf16[1,8,24,1024]{3,2,1,0:T(8,128)(2,1)S(1)} %collective-permute-done.near, bf16[1,8,24,1024]{3,2,1,0:T(8,128)(2,1)S(1)} %collective-permute-done.1.far, ...), custom_call_target="tpu_custom_call" | custom-call | tf_op jit(solution)/shard_map/join/pallas_call | solution.py:313
Async XLA Ops:
  5.4 19.1 %collective-permute-start.2 = (bf16[2,2,24,1024]{3,2,1,0:T(8,128)(2,1)S(1)}, bf16[2,2,24,1024]{3,2,1,0:T(8,128)(2,1)S(1)}, u32[]{:S(2)}, u32[]{:S(2)}) collective-permute-start(bf16[2,2,24,1024]{3,2,1,0:T(8,128)(2,1)S(1)} %get-tuple-element.19), channel_id=1, source_target_pairs={{0,1},{1,2},{2,3},{3,4},{4,5},{5,6},{6,7},{7,0},{8,9},{9,10},{10,1... | collective-permute-start | bytes 589832 | tf_op jit(solution)/shard_map/ppermute | solution.py:248
  7.1 17.4 %collective-permute-start.3 = (bf16[2,2,24,1024]{3,2,1,0:T(8,128)(2,1)S(1)}, bf16[2,2,24,1024]{3,2,1,0:T(8,128)(2,1)S(1)}, u32[]{:S(2)}, u32[]{:S(2)}) collective-permute-start(bf16[2,2,24,1024]{3,2,1,0:T(8,128)(2,1)S(1)} %get-tuple-element.20), channel_id=1, source_target_pairs={{0,7},{1,0},{2,1},{3,2},{4,3},{5,4},{6,5},{7,6},{8,15},{9,8},{10,9... | collective-permute-start | bytes 589832 | tf_op jit(solution)/shard_map/ppermute | solution.py:248
  10.3 14.2 %collective-permute-start = (bf16[1,8,24,1024]{3,2,1,0:T(8,128)(2,1)S(1)}, bf16[1,8,24,1024]{3,2,1,0:T(8,128)(2,1)S(1)}, u32[]{:S(2)}, u32[]{:S(2)}) collective-permute-start(bf16[1,8,24,1024]{3,2,1,0:T(8,128)(2,1)S(1)} %get-tuple-element.17), channel_id=1, source_target_pairs={{0,8},{8,0},{16,24},{24,16},{32,40},{40,32},{48,56},{56,48},{64,72... | collective-permute-start | bytes 1179656 | tf_op jit(solution)/shard_map/ppermute | solution.py:243
  11.3 13.2 %collective-permute-start.1 = (bf16[1,8,24,1024]{3,2,1,0:T(8,128)(2,1)S(1)}, bf16[1,8,24,1024]{3,2,1,0:T(8,128)(2,1)S(1)}, u32[]{:S(2)}, u32[]{:S(2)}) collective-permute-start(bf16[1,8,24,1024]{3,2,1,0:T(8,128)(2,1)S(1)} %get-tuple-element.18), channel_id=1, source_target_pairs={{0,0},{8,16},{16,8},{24,32},{32,24},{40,48},{48,40},{56,64},{64,56... | collective-permute-start | bytes 1179656 | tf_op jit(solution)/shard_map/ppermute | solution.py:243
